TPU v7x, 128 devices: a whole 4x4x4 slice. The times are simulated.
128 devices in a mesh: pool: 4 (over x), ep: 32 (over y, z, core).
Axes of the slice: x: 4, y: 4, z: 4, core: 2. Of those that a mesh axis runs over, the one named last changes fastest.
Arguments:
- tokens: bfloat16 [16384, 4096], P(('pool', 'ep')), may hold values from -6 to 6
- modality: int32 [16384], P(('pool', 'ep')), may hold values from 0 to 1, as said below
- chosen: int32 [32, 512], replicated, may hold values from 0 to 16383, as said below
- gates: float32 [32, 512], P('ep'), may hold values from 0.1 to 1
- w_gate: bfloat16 [32, 4096, 1024], P('ep', None, 'pool'), may hold values from -0.09375 to 0.09375
- w_up: bfloat16 [32, 4096, 1024], P('ep', None, 'pool'), may hold values from -0.09375 to 0.09375
- w_down: bfloat16 [32, 1024, 4096], P('ep', 'pool'), may hold values from -0.1875 to 0.1875
- cotangent: bfloat16 [16384, 4096], P(('pool', 'ep')), may hold values from -6 to 6
Outputs:
- mixed: bfloat16 [16384, 4096], P(('pool', 'ep'))
- token_grad: bfloat16 [16384, 4096], P(('pool', 'ep'))
- gate_grad: float32 [32, 512], P('ep')
- w_gate_grad: float32 [32, 4096, 1024], P('ep', None, 'pool')
- w_up_grad: float32 [32, 4096, 1024], P('ep', None, 'pool')
- w_down_grad: float32 [32, 1024, 4096], P('ep', 'pool')
Inputs may be any that keep to these rules, and one draw needn't show every extreme that they name: Every device's 128 tokens (device i holding tokens i * 128 to (i + 1) * 128 - 1) hold at least 8 tokens of each modality. `chosen`: row e lists 512 different tokens in increasing order; at most 8 of a row fall among one device's 128 tokens, and for every row exactly 8 do in some device.
All inputs are finite; a program needn't handle non-finite values.
Results may differ from a plain program's by a relative error of at most 0.0095.
Values may be sent and summed in bfloat16 or wider, within the bound.
No kernel may reach another device: no remote copies, remote signals or barrier semaphores. Data moves between devices by JAX's collectives and lax.ppermute only.
A program may use at most 128 MiB of HBM per device.

v0:
```python
import jax
import jax.numpy as jnp
from jax import lax
from jax.experimental import pallas as pl
from jax.experimental.pallas import tpu as pltpu
from jax.sharding import PartitionSpec as P

BF16 = jnp.bfloat16
F32 = jnp.float32
BOTH = ("pool", "ep")
ROW_COL = ((1,), (0,))
COL_COL = ((1,), (1,))
ROW_ROW = ((0,), (0,))


def dot(a, b, dims, out=F32):
    return lax.dot_general(a, b, (dims, ((), ())), preferred_element_type=out)


def add(*terms):
    total = terms[0].astype(F32)
    for term in terms[1:]:
        total = total + term.astype(F32)
    return total


def shift(value, step):
    size = lax.axis_size("pool")
    return lax.ppermute(value, "pool", [(i, (i + step) % size) for i in range(size)])


def after(value, *earlier):
    return lax.optimization_barrier((value, *earlier))[0]


def swap(get):
    behind = shift(get(-1), -1)
    before = shift(get(1), 1)
    far = shift(get(2), 2)
    return [get(0), behind, far, before]


def ring_gather(block):
    half = block.shape[0] // 2
    before, behind = shift(block, 1), shift(block, -1)
    far = shift(before[:half], 1), shift(behind[half:], -1)
    return [block, behind, far, before]


def thirds(value):
    high = lax.optimization_barrier(value.astype(BF16))
    rest = value - high.astype(F32)
    middle = lax.optimization_barrier(rest.astype(BF16))
    return high, middle, (rest - middle.astype(F32)).astype(BF16)


def kept(shape, dtype):
    return pltpu.HBM(shape, dtype)


def from_hbm(*arrays):
    return [pltpu.with_memory_space_constraint(array, pltpu.HBM) for array in arrays]


def whole_block(shape):
    return pl.BlockSpec(shape, lambda *index: (0,) * len(shape))


def params(megabytes):
    return pltpu.CompilerParams(vmem_limit_bytes=megabytes * 1024 * 1024)


def cost(flops, arrays):
    size = sum(int(array.size) * jnp.dtype(array.dtype).itemsize for array in arrays)
    return pl.CostEstimate(flops=int(flops), bytes_accessed=size, transcendentals=0)


def masked_send(pick, parts, text_rows):
    total, held = pick.shape
    rows = held // len(parts)
    cols = parts[0].shape[1]
    tile = total // 4

    def kernel(pick_ref, *refs):
        part_refs, out_ref, values, kinds = refs[: len(parts)], refs[-3], refs[-2], refs[-1]
        step = pl.program_id(0)

        @pl.when(step == 0)
        def _():
            for d, ref in enumerate(part_refs):
                values[d * rows : (d + 1) * rows, :] = ref[:rows, :]
                kinds[:, d * rows : (d + 1) * rows] = ref[rows:, :rows]

        kind = kinds[:1, :].astype(F32)
        row = step * tile + lax.broadcasted_iota(jnp.int32, (tile, 1), 0)
        keep = jnp.where(row < text_rows, 1.0 - kind, kind)
        chosen = (pick_ref[...].astype(F32) * keep).astype(BF16)
        out_ref[...] = dot(chosen, values[...], ROW_COL).astype(BF16)

    return pl.pallas_call(
        kernel,
        grid=(4,),
        out_shape=kept((total, cols), BF16),
        in_specs=[pl.BlockSpec((tile, held), lambda i: (i, 0))]
        + [pl.BlockSpec(part.shape, lambda i: (0, 0)) for part in parts],
        out_specs=pl.BlockSpec((tile, cols), lambda i: (i, 0)),
        scratch_shapes=[pltpu.VMEM((held, cols), BF16), pltpu.VMEM((16, held), BF16)],
        cost_estimate=pl.CostEstimate(
            flops=2 * total * held * cols, bytes_accessed=2 * (total * cols * 2 + total * held), transcendentals=0
        ),
        compiler_params=params(8),
    )(pick, *parts)


def assemble(parts, members, dtype, rows):
    cols = parts[0].shape[1]

    def kernel(members_ref, *refs):
        for d, ref in enumerate(refs[:-1]):
            start = pl.multiple_of(members_ref[d] * cols, 128)
            refs[-1][:, pl.ds(start, cols)] = ref[...].astype(dtype)

    return pl.pallas_call(
        kernel,
        grid_spec=pltpu.PrefetchScalarGridSpec(
            num_scalar_prefetch=1,
            grid=(2,),
            in_specs=[pl.BlockSpec((rows // 2, cols), lambda i, m: (i, 0)) for _ in parts],
            out_specs=pl.BlockSpec((rows // 2, len(parts) * cols), lambda i, m: (i, 0)),
        ),
        out_shape=jax.ShapeDtypeStruct((rows, len(parts) * cols), dtype),
        cost_estimate=pl.CostEstimate(
            flops=0, bytes_accessed=len(parts) * rows * cols * (2 + jnp.dtype(dtype).itemsize), transcendentals=0
        ),
        compiler_params=params(10),
    )(members, *parts)


def weight_grads(inputs, members, gate_back, up_back):
    count, cols = inputs[0].shape
    share = gate_back.shape[1]
    blocks = [block if isinstance(block, tuple) else (block,) for block in inputs]
    pieces = [piece for block in blocks for piece in block]

    def kernel(members_ref, *refs):
        gate_ref, up_ref, gate_out, up_out = refs[-4:]
        refs = list(refs[: len(pieces)])
        for d, block in enumerate(blocks):
            held = [refs.pop(0) for _ in block]

            @pl.when(pl.program_id(0) == d)
            def _(held=held):
                for grad, out in ((gate_ref, gate_out), (up_ref, up_out)):
                    size = held[0].shape[0]
                    out[...] = sum(
                        dot(ref[...], grad[i * size : (i + 1) * size, :], ROW_ROW) for i, ref in enumerate(held)
                    )

    whole = jax.ShapeDtypeStruct((len(inputs) * cols, share), F32)
    return pl.pallas_call(
        kernel,
        grid_spec=pltpu.PrefetchScalarGridSpec(
            num_scalar_prefetch=1,
            grid=(len(inputs),),
            in_specs=[whole_block(piece.shape) for piece in pieces] + [whole_block((count, share))] * 2,
            out_specs=[pl.BlockSpec((cols, share), lambda d, m: (m[d], 0))] * 2,
        ),
        out_shape=[whole, whole],
        cost_estimate=pl.CostEstimate(
            flops=4 * count * cols * share * len(inputs),
            bytes_accessed=len(inputs) * (count * cols * 2 + cols * share * 8),
            transcendentals=0,
        ),
        compiler_params=params(16),
    )(members, *pieces, gate_back, up_back)


def hidden_from(gate_sum, up_sum, far, w_gate, w_up, members):
    half, cols = far[0].shape
    count, share = gate_sum.shape

    def kernel(members_ref, gate_ref, up_ref, top, low, wg_ref, wu_ref, gate_out, up_out, hidden_out):
        for start, ref in ((0, top), (half, low)):
            span = slice(start, start + half)
            gate = gate_ref[span, :] + dot(ref[...], wg_ref[...], ROW_COL)
            up = up_ref[span, :] + dot(ref[...], wu_ref[...], ROW_COL)
            gate_out[span, :] = gate
            up_out[span, :] = up
            hidden_out[span, :] = (gate * jax.nn.sigmoid(gate) * up).astype(BF16)

    wide = kept((count, share), F32)
    return pl.pallas_call(
        kernel,
        grid_spec=pltpu.PrefetchScalarGridSpec(
            num_scalar_prefetch=1,
            grid=(1,),
            in_specs=[whole_block((count, share))] * 2
            + [whole_block((half, cols))] * 2
            + [pl.BlockSpec((cols, share), lambda i, m: (m[2], 0))] * 2,
            out_specs=[whole_block((count, share))] * 3,
        ),
        out_shape=[wide, wide, jax.ShapeDtypeStruct((count, share), BF16)],
        cost_estimate=cost(4 * count * cols * share, (gate_sum, up_sum, *far, gate_sum, up_sum)),
        compiler_params=params(8),
    )(members, gate_sum, up_sum, *far, w_gate, w_up)


def fetch_and_back(place_in, got, down_parts):
    count, total = place_in.shape
    share, cols = down_parts[0].shape
    tile = count // 2

    def kernel(place_ref, got_ref, *refs):
        downs, (rows_out, *back_out) = refs[: len(down_parts)], refs[len(down_parts) :]
        rows = dot(place_ref[...], got_ref[...], ROW_COL).astype(BF16)
        rows_out[...] = rows
        for down, out in zip(downs, back_out):
            out[...] = dot(rows, down[...], COL_COL).astype(out.dtype)

    kinds = [F32] + [BF16] * (len(down_parts) - 1)
    return pl.pallas_call(
        kernel,
        grid=(2,),
        in_specs=[pl.BlockSpec((tile, total), lambda i: (i, 0)), whole_block(got.shape)]
        + [whole_block((share, cols))] * len(down_parts),
        out_specs=[pl.BlockSpec((tile, cols), lambda i: (i, 0))]
        + [pl.BlockSpec((tile, share), lambda i: (i, 0))] * len(kinds),
        out_shape=[kept((count, cols), BF16)]
        + [jax.ShapeDtypeStruct((count, share), kind) for kind in kinds],
        cost_estimate=cost(2 * count * total * cols + 8 * count * share * cols, (place_in, got, *down_parts)),
        compiler_params=params(14),
    )(*from_hbm(place_in, got, *down_parts))


def weighted_slots(hidden_parts, down_parts, weight, place_out):
    total, count = place_out.shape
    share, cols = down_parts[0].shape
    tile = cols // 4
    pieces = len(hidden_parts)

    def kernel(*refs):
        hiddens, downs = refs[:pieces], refs[pieces : 2 * pieces]
        weight_ref, place_ref, slots_out = refs[2 * pieces :]
        hidden = jnp.concatenate([ref[...] for ref in hiddens], axis=1)
        out = dot(hidden, jnp.concatenate([ref[...] for ref in downs], axis=0), ROW_COL)
        slots_out[...] = dot(place_ref[...], (weight_ref[...] * out).astype(BF16), ROW_COL).astype(BF16)

    return pl.pallas_call(
        kernel,
        grid=(4,),
        in_specs=[whole_block((count, share))] * pieces
        + [pl.BlockSpec((share, tile), lambda i: (0, i))] * pieces
        + [whole_block((count, 1)), whole_block((total, count))],
        out_specs=pl.BlockSpec((total, tile), lambda i: (0, i)),
        out_shape=kept((total, cols), BF16),
        cost_estimate=cost(
            2 * count * cols * (total + pieces * share), (*hidden_parts, *down_parts, place_out, place_out)
        ),
        compiler_params=params(10),
    )(*hidden_parts, *down_parts, weight, place_out)


def first_hop(back_parts, hidden, gate_pre, up_pre, weight, w_gate, w_up, order):
    count, share = gate_pre.shape
    half = count // 2
    cols = w_gate.shape[0] // (len(order) + 1)
    pieces = len(back_parts)

    def kernel(order_ref, *refs):
        hidden_ref, gate_ref, up_ref, weight_ref, wg_ref, wu_ref = refs[pieces : pieces + 6]
        gate_out, up_out, rise_out, fall_out, sum_out = refs[pieces + 6 :]
        step = pl.program_id(0)

        @pl.when(step == 0)
        def _():
            back = add(*(ref[...] for ref in refs[:pieces]))
            sum_out[...] = jnp.sum(hidden_ref[...].astype(F32) * back, axis=1, keepdims=True)
            back = weight_ref[...] * back
            gate = gate_ref[...]
            sig = jax.nn.sigmoid(gate)
            gate_out[...] = (back * up_ref[...] * (sig * (1.0 + gate * (1.0 - sig)))).astype(BF16)
            up_out[...] = (back * (gate * sig)).astype(BF16)

        def product(start, stop):
            grads = jnp.concatenate([gate_out[start:stop, :], up_out[start:stop, :]], axis=1)
            weights = jnp.concatenate([wg_ref[...], wu_ref[...]], axis=1)
            return dot(grads, weights, COL_COL).astype(BF16)

        @pl.when(step == 0)
        def _():
            rows = product(0, count)
            rise_out[:half, :] = rows[:half]
            fall_out[half:, :] = rows[half:]

        @pl.when(step == 1)
        def _():
            rise_out[half:, :] = product(half, count)

        @pl.when(step == 2)
        def _():
            fall_out[:half, :] = product(0, half)

    small = kept((count, share), BF16)
    wide = kept((count, cols), BF16)
    return pl.pallas_call(
        kernel,
        grid_spec=pltpu.PrefetchScalarGridSpec(
            num_scalar_prefetch=1,
            grid=(len(order),),
            in_specs=[whole_block((count, share))] * (pieces + 3)
            + [whole_block((count, 1))]
            + [pl.BlockSpec((cols, share), lambda j, m: (m[j], 0))] * 2,
            out_specs=[whole_block((count, share))] * 2
            + [whole_block((count, cols))] * 2
            + [whole_block((count, 1))],
        ),
        out_shape=[small, small, wide, wide, kept((count, 1), F32)],
        cost_estimate=cost(8 * count * share * cols, (*back_parts, gate_pre, up_pre, w_gate, w_up)),
        compiler_params=params(16),
    )(jnp.stack(order).astype(jnp.int32), *back_parts, hidden, *from_hbm(gate_pre, up_pre, weight, w_gate, w_up))


def summed_slots(own, rise, fall, rise_last, fall_last, place_out):
    total, count = place_out.shape
    half, cols = rise_last.shape
    tile = cols // 4

    def kernel(own_ref, rise_ref, fall_ref, rise_last_ref, fall_last_ref, place_ref, out_ref):
        top = add(own_ref[:half, :], rise_last_ref[...], fall_ref[...])
        low = add(own_ref[half:, :], rise_ref[...], fall_last_ref[...])
        sums = jnp.concatenate([top, low], axis=0).astype(BF16)
        out_ref[...] = dot(place_ref[...], sums, ROW_COL).astype(BF16)

    return pl.pallas_call(
        kernel,
        grid=(4,),
        in_specs=[
            pl.BlockSpec((count, tile), lambda i: (0, i)),
            pl.BlockSpec((half, tile), lambda i: (1, i)),
            pl.BlockSpec((half, tile), lambda i: (0, i)),
            pl.BlockSpec((half, tile), lambda i: (0, i)),
            pl.BlockSpec((half, tile), lambda i: (0, i)),
            whole_block((total, count)),
        ],
        out_specs=pl.BlockSpec((total, tile), lambda i: (0, i)),
        out_shape=kept((total, cols), BF16),
        cost_estimate=cost(2 * total * count * cols, (own, rise, fall, place_out, place_out)),
        compiler_params=params(10),
    )(own, rise, fall, rise_last, fall_last, place_out)


def body(tokens, modality, chosen, gates, w_gate, w_up, w_down, cotangent):
    tok_rows, width = tokens.shape
    size = lax.axis_size("pool")
    ep_size = lax.axis_size("ep")
    slots = 2 * tok_rows // ep_size
    capacity = chosen.shape[1]
    text_count = 3 * ep_size // 4
    cols = width // size
    share = w_gate.shape[2]
    me = lax.axis_index("pool")
    mine = lax.axis_index("ep")
    members = [(me + d) % size for d in range(size)]
    pool_order = jnp.stack(members).astype(jnp.int32)

    def columns(array):
        return lambda d: lax.dynamic_slice(
            array, (0, members[d % size] * cols), (array.shape[0], cols)
        )

    def rows(array, count):
        return lambda d: lax.dynamic_slice(
            array, (members[d % size] * count, 0), (count, array.shape[1])
        )

    extra = jnp.broadcast_to(jnp.pad(modality, (0, cols - tok_rows)).astype(BF16), (16, cols))
    token_parts = swap(lambda d: jnp.concatenate([columns(tokens)(d), extra], axis=0))
    later = token_parts[1:]
    grad_parts = swap(lambda d: after(columns(cotangent)(d), *later) if d == 2 else columns(cotangent)(d))
    down_parts = swap(lambda d: after(columns(w_down[0])(d), *later))

    token_at = []
    for d in range(size):
        first = (members[d] * ep_size + mine) * tok_rows
        local = chosen - first
        below = jnp.sum((local < 0).astype(jnp.int32), axis=1, keepdims=True)
        inside = (local >= 0) & (local < tok_rows)
        place = jnp.where(inside, jnp.arange(capacity, dtype=jnp.int32)[None, :] - below, -1)
        at_slot = place[:, None, :] == jnp.arange(slots, dtype=jnp.int32)[None, :, None]
        held = jnp.sum(jnp.where(at_slot, local[:, None, :] + 1, 0), axis=2) - 1
        token_at.append(jnp.where(held < 0, -1, held + d * tok_rows))
    token_at = jnp.stack(token_at, axis=1).reshape(ep_size * size * slots, 1)
    token_ids = jnp.arange(size * tok_rows, dtype=jnp.int32)
    pick = (token_at == token_ids[None, :]).astype(BF16)
    pick_back = (token_at.reshape(1, -1) == token_ids[:, None]).astype(BF16)
    pick, pick_back = lax.optimization_barrier((pick, pick_back))

    picks = lax.dynamic_slice_in_dim(chosen, mine, 1, 0)[0]
    holder = picks // tok_rows
    order = jnp.arange(capacity, dtype=jnp.int32)
    same = (holder[:, None] == holder[None, :]) & (order[None, :] < order[:, None])
    rank = jnp.sum(same.astype(jnp.int32), axis=1)
    pool_of, ep_of = holder // ep_size, holder % ep_size
    flat = (ep_of * size + (pool_of - me) % size) * slots + rank
    slot_total = ep_size * size * slots
    slot_ids = jnp.arange(slot_total, dtype=jnp.int32)
    place_in = (flat[:, None] == slot_ids[None, :]).astype(BF16)
    place_out = (flat[None, :] == slot_ids[:, None]).astype(BF16)
    place_in, place_out = lax.optimization_barrier((place_in, place_out))

    def exchange(values):
        blocks = values.reshape(ep_size, size * slots, cols)
        blocks = lax.all_to_all(blocks, "ep", split_axis=0, concat_axis=0, tiled=True)
        return blocks.reshape(slot_total, cols)

    def fetch(got):
        return dot(place_in, got, ROW_COL, BF16)

    def collect(got):
        return dot(pick_back, got, ROW_COL, BF16)

    def of_holder(summed, d):
        return summed[d % size * tok_rows : (d % size + 1) * tok_rows]

    wg, wu = w_gate[0], w_up[0]
    weight = gates[0][:, None]
    sent = masked_send(pick, token_parts, text_count * size * slots)
    sent_grads = dot(pick, jnp.concatenate(grad_parts, axis=0), ROW_COL, BF16)
    block = fetch(after(exchange(after(sent, grad_parts[1], grad_parts[3])), sent_grads))
    inputs = ring_gather(block)
    got = exchange(after(sent_grads, block, *down_parts))

    def near_sum(weights):
        return sum(dot(inputs[d], rows(weights, cols)(d), ROW_COL) for d in (0, 1, 3))

    gate_pre, up_pre, hidden = hidden_from(near_sum(wg), near_sum(wu), inputs[2], wg, wu, pool_order)
    grads, *back_parts = fetch_and_back(place_in, got, down_parts)
    came = swap(lambda d: back_parts[d % size])
    hidden_parts = swap(lambda d: hidden)
    hidden_parts = lax.optimization_barrier((*hidden_parts, *back_parts))[:size]

    slots_out = weighted_slots(hidden_parts, down_parts, weight, place_out)
    came[1] = after(came[1], slots_out)
    gate_back, up_back, rise, fall, gate_sum = first_hop(
        came, hidden, gate_pre, up_pre, weight, wg, wu, [members[2], members[1], members[3]]
    )
    sent_first = rise, fall
    mixed_sum = collect(exchange(after(slots_out, *sent_first)))
    rise, fall = shift(rise, 1), shift(fall, -1)
    half = capacity // 2

    def share_in(d, span):
        gate, up = (after(grad, *sent_first)[span] for grad in (gate_back, up_back))
        return dot(gate, rows(wg, cols)(d), COL_COL) + dot(up, rows(wu, cols)(d), COL_COL)

    own = share_in(0, slice(None))
    hops = (
        (share_in(1, slice(0, half)) + rise[:half].astype(F32)).astype(BF16),
        (share_in(3, slice(half, None)) + fall[half:].astype(F32)).astype(BF16),
    )
    last = shift(hops[0], 1), shift(hops[1], -1)
    slots_in = summed_slots(own, rise, fall, *last, place_out)
    got = exchange(slots_in)

    gate_sum = after(gate_sum, *hops).reshape(1, capacity)
    gate_rows = jnp.concatenate(thirds(gate_sum), axis=0)
    gate_rows = jnp.pad(gate_rows, ((0, 13), (0, cols - capacity)))
    mixed_parts = swap(lambda d: jnp.concatenate([of_holder(mixed_sum, d), gate_rows], axis=0))
    mixed = assemble(mixed_parts, pool_order, BF16, tok_rows)
    gate_parts = [part[tok_rows : tok_rows + 3, :capacity].astype(F32) for part in mixed_parts]
    gate_parts = [part[0:1] + part[1:2] + part[2:3] for part in gate_parts]
    gate_grad = (gate_parts[0] + gate_parts[2]) + (gate_parts[1] + gate_parts[3])
    hidden_all = jnp.concatenate(after(hidden_parts, *hops), axis=1)
    scaled = (weight * hidden_all.astype(F32)).astype(BF16)
    down_grad = dot(scaled, grads, ROW_ROW, BF16)

    def down_block(d):
        block = down_grad[d % size * share : (d % size + 1) * share]
        return after(block, *last) if d == 2 else block

    down_grad = swap(down_block)
    down_grad = [after(part, mixed_sum) for part in down_grad]
    wd_grad = assemble(down_grad, pool_order, F32, share)
    wg_grad, wu_grad = weight_grads(
        inputs, pool_order, after(gate_back, slots_in, mixed_sum), after(up_back, slots_in)
    )
    got = after(got, mixed, wd_grad, wg_grad, wu_grad, gate_grad)
    summed = collect(got)
    token_grad = assemble(swap(lambda d: of_holder(summed, d)), pool_order, BF16, tok_rows)
    return (mixed, token_grad, gate_grad, wg_grad[None], wu_grad[None], wd_grad[None])


def solution(mesh):
    return jax.shard_map(
        body,
        mesh=mesh,
        in_specs=(
            P(BOTH, None),
            P(BOTH),
            P(),
            P("ep", None),
            P("ep", None, "pool"),
            P("ep", None, "pool"),
            P("ep", "pool", None),
            P(BOTH, None),
        ),
        out_specs=(
            P(BOTH, None),
            P(BOTH, None),
            P("ep", None),
            P("ep", None, "pool"),
            P("ep", None, "pool"),
            P("ep", "pool", None),
        ),
        check_vma=False,
    )
```

profile of v0, /device:TPU:0, one launch (start us, length us, event | category | flops | bytes accessed | tf_op | source)
XLA Modules:
  0.0 254.4 jit_solution(16574569957711352346)
XLA Ops:
  2.8 2.9 %collective-permute-start = (bf16[144,1024]{1,0:T(8,128)(2,1)S(1)}, bf16[144,1024]{1,0:T(8,128)(2,1)S(1)}, u32[]{:S(2)}, u32[]{:S(2)}) collective-permute-start(bf16[144,1024]{1,0:T(8,128)(2,1)S(1)} %get-tuple-element.143), channel_id=1, source_target_pairs={{0,96},{32,0},{64,32},{96,64},{1,97},{33,1},{65,33},{97,65},{2,98}... | collective-permute-start | bytes 884744 | tf_op jit(solution)/shard_map/ppermute | solution.py:29
  8.3 1.8 collective-permute-start.4
  15.9 3.4 %collective-permute-done.refs_1_ = bf16[144,1024]{1,0:T(8,128)(2,1)S(1)} collective-permute-done((bf16[144,1024]{1,0:T(8,128)(2,1)S(1)}, bf16[144,1024]{1,0:T(8,128)(2,1)S(1)}, u32[]{:S(2)}, u32[]{:S(2)}) %collective-permute-start) | collective-permute-done | bytes 294944 | tf_op jit(solution)/shard_map/ppermute | solution.py:29
  19.3 2.8 %collective-permute-done.2.refs_3_ = bf16[144,1024]{1,0:T(8,128)(2,1)S(1)} collective-permute-done((bf16[144,1024]{1,0:T(8,128)(2,1)S(1)}, bf16[144,1024]{1,0:T(8,128)(2,1)S(1)}, u32[]{:S(2)}, u32[]{:S(2)}) %collective-permute-start.2) | collective-permute-done | bytes 294944 | tf_op jit(solution)/shard_map/ppermute | solution.py:29
  22.1 3.0 %shard_map.127 = bf16[1024,1024]{1,0:T(8,128)(2,1)} custom-call(bf16[1024,512]{1,0:T(8,128)(2,1)S(1)} %fusion.pick_ref, bf16[144,1024]{1,0:T(8,128)(2,1)S(1)} %get-tuple-element.142.refs_0_, bf16[144,1024]{1,0:T(8,128)(2,1)S(1)} %collective-permute-done.refs_1_, bf16[144,1024]{1,0:T(8,128)(2,1)S(1)} %collective-permute-done.1.refs_2_, ...), custom_call_target="tpu_custom_call" | custom-call | flops 1073741824 | bytes 5242880 | tf_op jit(solution)/shard_map/pallas_call | solution.py:100
  25.2 2.6 %collective-permute-done.4 = bf16[128,1024]{1,0:T(8,128)(2,1)} collective-permute-done((bf16[128,1024]{1,0:T(8,128)(2,1)}, bf16[128,1024]{1,0:T(8,128)(2,1)}, u32[]{:S(2)}, u32[]{:S(2)}) %collective-permute-start.4) | collective-permute-done | bytes 262176 | tf_op jit(solution)/shard_map/ppermute | solution.py:29
  27.8 8.5 %all-to-all-start = ((bf16[32,32,1024]{2,1,0:T(8,128)(2,1)}), bf16[32,32,1024]{2,1,0:T(8,128)(2,1)}, u32[]{:S(2)}, u32[]{:S(2)}) async-start(bf16[32,32,1024]{2,1,0:T(8,128)(2,1)} %bitcast.94), calls=%async_computation | async-start | bytes 4194304 | tf_op jit(solution)/shard_map/all_to_all | solution.py:413
  41.4 2.7 %collective-permute-start.14 = (bf16[256,1024]{1,0:T(8,128)(2,1)}, bf16[256,1024]{1,0:T(8,128)(2,1)S(1)}, u32[]{:S(2)}, u32[]{:S(2)}) collective-permute-start(bf16[256,1024]{1,0:T(8,128)(2,1)} %get-tuple-element.63), channel_id=1, source_target_pairs={{0,64},{32,96},{64,0},{96,32},{1,65},{33,97},{65,1},{97,33},{2,66}... | collective-permute-start | bytes 1572872 | tf_op jit(solution)/shard_map/ppermute | solution.py:29
  46.2 2.8 %collective-permute-done.5 = bf16[128,1024]{1,0:T(8,128)(2,1)S(1)} collective-permute-done((bf16[128,1024]{1,0:T(8,128)(2,1)}, bf16[128,1024]{1,0:T(8,128)(2,1)S(1)}, u32[]{:S(2)}, u32[]{:S(2)}) %collective-permute-start.5) | collective-permute-done | bytes 262176 | tf_op jit(solution)/shard_map/ppermute | solution.py:29
  49.0 3.7 %fusion.5 = bf16[1024,1024]{1,0:T(8,128)(2,1)} fusion(bf16[1024,512]{1,0:T(8,128)(2,1)S(1)} %fusion.pick_ref, bf16[128,1024]{1,0:T(8,128)(2,1)} %collective-permute-done.4, bf16[128,1024]{1,0:T(8,128)(2,1)S(1)} %collective-permute-done.5, bf16[128,1024]{1,0:T(8,128)(2,1)} %collective-permute-done.3, bf16[128,1024]{1,0:T(8,128)(2,1)S(1)} %get-tuple-element.130), kind=kOutput, calls=%fused_computation.17 | convolution fusion | flops 1077936128 | bytes 4194304 | tf_op jit(solution)/shard_map/dot_general | solution.py:17
  52.7 12.5 %all-to-all-done = bf16[32,32,1024]{2,1,0:T(8,128)(2,1)} async-done(((bf16[32,32,1024]{2,1,0:T(8,128)(2,1)}), bf16[32,32,1024]{2,1,0:T(8,128)(2,1)}, u32[]{:S(2)}, u32[]{:S(2)}) %all-to-all-start) | async-done | bytes 2097184 | tf_op jit(solution)/shard_map/all_to_all | solution.py:413
  65.2 3.9 %fusion.99.refs_0_ = bf16[512,1024]{1,0:T(8,128)(2,1)} fusion(bf16[512,1024]{1,0:T(8,128)(2,1)S(1)} %copy-done.27, bf16[1024,1024]{1,0:T(8,128)(2,1)} %bitcast.13), kind=kOutput, calls=%fused_computation.200 | convolution fusion | flops 1073741824 | bytes 4194304 | tf_op jit(solution)/shard_map/dot_general | solution.py:17
  69.1 3.2 %collective-permute-start.6 = (bf16[512,1024]{1,0:T(8,128)(2,1)}, bf16[512,1024]{1,0:T(8,128)(2,1)}, u32[]{:S(2)}, u32[]{:S(2)}) collective-permute-start(bf16[512,1024]{1,0:T(8,128)(2,1)} %fusion.99.refs_0_), channel_id=1, source_target_pairs={{0,96},{32,0},{64,32},{96,64},{1,97},{33,1},{65,33},{97,65},{2,98}... | collective-permute-start | bytes 3145736 | tf_op jit(solution)/shard_map/ppermute | solution.py:29
  73.3 5.3 %all-to-all-start.1 = ((bf16[32,32,1024]{2,1,0:T(8,128)(2,1)}), bf16[32,32,1024]{2,1,0:T(8,128)(2,1)}, u32[]{:S(2)}, u32[]{:S(2)}) async-start(bf16[32,32,1024]{2,1,0:T(8,128)(2,1)} %bitcast.98), calls=%async_computation.1 | async-start | bytes 4194304 | tf_op jit(solution)/shard_map/all_to_all | solution.py:413
  82.1 13.1 %collective-permute-done.7.refs_4_ = bf16[512,1024]{1,0:T(8,128)(2,1)S(1)} collective-permute-done((bf16[512,1024]{1,0:T(8,128)(2,1)}, bf16[512,1024]{1,0:T(8,128)(2,1)S(1)}, u32[]{:S(2)}, u32[]{:S(2)}) %collective-permute-start.7) | collective-permute-done | bytes 1048608 | tf_op jit(solution)/shard_map/ppermute | solution.py:29
  96.4 3.3 %collective-permute-start.9 = (bf16[256,1024]{1,0:T(8,128)(2,1)S(1)}, bf16[256,1024]{1,0:T(8,128)(2,1)S(1)}, u32[]{:S(2)}, u32[]{:S(2)}) collective-permute-start(bf16[256,1024]{1,0:T(8,128)(2,1)S(1)} %slice.142), channel_id=1, source_target_pairs={{0,96},{32,0},{64,32},{96,64},{1,97},{33,1},{65,33},{97,65},{2,98}... | collective-permute-start | bytes 1572872 | tf_op jit(solution)/shard_map/ppermute | solution.py:29
  103.9 5.2 %collective-permute-done.8.top.refs_2_ = bf16[256,1024]{1,0:T(8,128)(2,1)S(1)} collective-permute-done((bf16[256,1024]{1,0:T(8,128)(2,1)S(1)}, bf16[256,1024]{1,0:T(8,128)(2,1)S(1)}, u32[]{:S(2)}, u32[]{:S(2)}) %collective-permute-start.8) | collective-permute-done | bytes 524320 | tf_op jit(solution)/shard_map/ppermute | solution.py:29
  109.6 2.2 shard_map.128
  112.1 5.2 %collective-permute-start.11 = (bf16[512,256]{1,0:T(8,128)(2,1)S(1)}, bf16[512,256]{1,0:T(8,128)(2,1)}, u32[]{:S(2)}, u32[]{:S(2)}) collective-permute-start(bf16[512,256]{1,0:T(8,128)(2,1)S(1)} %get-tuple-element.87.refs_0_.refs_4_), channel_id=1, source_target_pairs={{0,64},{32,96},{64,0},{96,32},{1,65},{33,97},{65,1},{97,33},{2,66}... | collective-permute-start | bytes 786440 | tf_op jit(solution)/shard_map/ppermute | solution.py:29
  117.3 5.5 %shard_map.129 = (bf16[512,1024]{1,0:T(8,128)(2,1)}, f32[512,256]{1,0:T(8,128)S(1)}, bf16[512,256]{1,0:T(8,128)(2,1)S(1)}, bf16[512,256]{1,0:T(8,128)(2,1)S(1)}, bf16[512,256]{1,0:T(8,128)(2,1)S(1)}) custom-call(bf16[512,1024]{1,0:T(8,128)(2,1)} %fusion.2.place_ref, bf16[1024,1024]{1,0:T(8,128)(2,1)} %bitcast.27.got_ref, ...), custom_call_target="tpu_custom_call" | custom-call | flops 2147483648 | bytes 5242880 | tf_op jit(solution)/shard_map/pallas_call | solution.py:221
  122.9 2.0 collective-permute-start.18
  125.0 2.6 %collective-permute-start.16 = (bf16[512,256]{1,0:T(8,128)(2,1)S(1)}, bf16[512,256]{1,0:T(8,128)(2,1)S(1)}, u32[]{:S(2)}, u32[]{:S(2)}) collective-permute-start(bf16[512,256]{1,0:T(8,128)(2,1)S(1)} %get-tuple-element.69), channel_id=1, source_target_pairs={{0,96},{32,0},{64,32},{96,64},{1,97},{33,1},{65,33},{97,65},{2,98}... | collective-permute-start | bytes 786440 | tf_op jit(solution)/shard_map/ppermute | solution.py:29
  127.7 2.4 collective-permute-done.11.refs_2_
  130.2 7.3 %shard_map.130 = bf16[1024,1024]{1,0:T(8,128)(2,1)} custom-call(bf16[512,256]{1,0:T(8,128)(2,1)S(1)} %get-tuple-element.87.refs_0_.refs_4_, bf16[512,256]{1,0:T(8,128)(2,1)} %collective-permute-done.10.refs_1_, bf16[512,256]{1,0:T(8,128)(2,1)} %collective-permute-done.11.refs_2_, bf16[512,256]{1,0:T(8,128)(2,1)S(1)} %collective-permute-done.12.refs_3_, ...), custom_call_target="tpu_custom_call" | custom-call | flops 2147483648 | bytes 5242880 | tf_op jit(solution)/shard_map/pallas_call | solution.py:248
  137.8 6.3 %shard_map.131 = (bf16[512,256]{1,0:T(8,128)(2,1)}, bf16[512,256]{1,0:T(8,128)(2,1)}, bf16[512,1024]{1,0:T(8,128)(2,1)}, bf16[512,1024]{1,0:T(8,128)(2,1)}, f32[512,1]{1,0:T(8,128)}) custom-call(s32[3]{0:T(128)S(1)} %pad_add_fusion.2.order_ref, f32[512,256]{1,0:T(8,128)S(1)} %get-tuple-element.66.refs_0_, ...), custom_call_target="tpu_custom_call" | custom-call | flops 1073741824 | bytes 6553600 | tf_op jit(solution)/shard_map/pallas_call | solution.py:305
  144.2 2.0 collective-permute-start.19
  146.2 2.1 collective-permute-start.20
  148.3 6.8 %all-to-all-start.2 = ((bf16[32,32,1024]{2,1,0:T(8,128)(2,1)}), bf16[32,32,1024]{2,1,0:T(8,128)(2,1)}, u32[]{:S(2)}, u32[]{:S(2)}) async-start(bf16[32,32,1024]{2,1,0:T(8,128)(2,1)} %bitcast.97), calls=%async_computation.2 | async-start | bytes 4194304 | tf_op jit(solution)/shard_map/all_to_all | solution.py:413
  159.2 9.8 %collective-permute-done.19.rise_ref = bf16[512,1024]{1,0:T(8,128)(2,1)} collective-permute-done((bf16[512,1024]{1,0:T(8,128)(2,1)}, bf16[512,1024]{1,0:T(8,128)(2,1)}, u32[]{:S(2)}, u32[]{:S(2)}) %collective-permute-start.19) | collective-permute-done | bytes 1048608 | tf_op jit(solution)/shard_map/ppermute | solution.py:29
  169.0 2.2 add_convert_fusion.1
  171.6 2.2 add_convert_fusion
  173.7 2.9 %collective-permute-start.25 = (bf16[256,1024]{1,0:T(8,128)(2,1)}, bf16[256,1024]{1,0:T(8,128)(2,1)}, u32[]{:S(2)}, u32[]{:S(2)}) collective-permute-start(bf16[256,1024]{1,0:T(8,128)(2,1)} %add_convert_fusion), channel_id=1, source_target_pairs={{0,96},{32,0},{64,32},{96,64},{1,97},{33,1},{65,33},{97,65},{2,98}... | collective-permute-start | bytes 1572872 | tf_op jit(solution)/shard_map/ppermute | solution.py:29
  176.8 2.8 %fusion.4 = bf16[1024,1024]{1,0:T(8,128)(2,1)S(1)} fusion(bf16[512,1024]{1,0:T(8,128)(2,1)} %get-tuple-element.91, bf16[512,256]{1,0:T(8,128)(2,1)S(1)} %copy-done.23, bf16[512,256]{1,0:T(8,128)(2,1)} %collective-permute-done.11.refs_2_, bf16[512,256]{1,0:T(8,128)(2,1)} %collective-permute-done.10.refs_1_, bf16[512,256]{1,0:T(8,128)(2,1)S(1)} %copy-done.17, ...), kind=kOutput, calls=%fused_computation.16 | convolution fusion | flops 1078984704 | bytes 4196352 | tf_op jit(solution)/shard_map/dot_general | solution.py:17
  180.8 3.2 %collective-permute-start.26 = (bf16[256,1024]{1,0:T(8,128)(2,1)}, bf16[256,1024]{1,0:T(8,128)(2,1)S(1)}, u32[]{:S(2)}, u32[]{:S(2)}) collective-permute-start(bf16[256,1024]{1,0:T(8,128)(2,1)} %get-tuple-element.112), channel_id=1, source_target_pairs={{0,96},{32,0},{64,32},{96,64},{1,97},{33,1},{65,33},{97,65},{2,98}... | collective-permute-start | bytes 1572872 | tf_op jit(solution)/shard_map/ppermute | solution.py:29
  185.0 3.9 %collective-permute-done.25.fall_last_ref = bf16[256,1024]{1,0:T(8,128)(2,1)} collective-permute-done((bf16[256,1024]{1,0:T(8,128)(2,1)}, bf16[256,1024]{1,0:T(8,128)(2,1)}, u32[]{:S(2)}, u32[]{:S(2)}) %collective-permute-start.25) | collective-permute-done | bytes 524320 | tf_op jit(solution)/shard_map/ppermute | solution.py:29
  188.9 4.8 %shard_map.133 = bf16[1024,1024]{1,0:T(8,128)(2,1)} custom-call(f32[512,1024]{1,0:T(8,128)S(1)} %copy-done.4, bf16[512,1024]{1,0:T(8,128)(2,1)} %collective-permute-done.19.rise_ref, bf16[512,1024]{1,0:T(8,128)(2,1)} %collective-permute-done.20.fall_ref, bf16[256,1024]{1,0:T(8,128)(2,1)S(1)} %collective-permute-done.24.rise_last_ref, ...), custom_call_target="tpu_custom_call" | custom-call | flops 1073741824 | bytes 6291456 | tf_op jit(solution)/shard_map/pallas_call | solution.py:334
  193.8 9.0 %all-to-all-start.3 = ((bf16[32,32,1024]{2,1,0:T(8,128)(2,1)}), bf16[32,32,1024]{2,1,0:T(8,128)(2,1)}, u32[]{:S(2)}, u32[]{:S(2)}) async-start(bf16[32,32,1024]{2,1,0:T(8,128)(2,1)} %bitcast.95), calls=%async_computation.3 | async-start | bytes 4194304 | tf_op jit(solution)/shard_map/all_to_all | solution.py:413
  202.8 2.5 collective-permute-start.27
  205.3 3.2 %fusion.100 = bf16[512,1024]{1,0:T(8,128)(2,1)S(1)} fusion(bf16[512,1024]{1,0:T(8,128)(2,1)} %fusion.1, bf16[1024,1024]{1,0:T(8,128)(2,1)} %bitcast.30), kind=kOutput, calls=%fused_computation.201 | convolution fusion | flops 1073741824 | bytes 4194304 | tf_op jit(solution)/shard_map/dot_general | solution.py:17
  208.8 2.2 collective-permute-start.23
  213.1 7.1 %shard_map.135 = (f32[4096,256]{1,0:T(8,128)}, f32[4096,256]{1,0:T(8,128)}) custom-call(s32[4]{0:T(128)S(1)} %pad_add_fusion.1.members_ref, bf16[512,1024]{1,0:T(8,128)(2,1)} %fusion.99.refs_0_, bf16[512,1024]{1,0:T(8,128)(2,1)} %collective-permute-done.6.refs_1_, bf16[256,1024]{1,0:T(8,128)(2,1)S(1)} %copy-done.12, bf16[256,1024]{1,0:T(8,128)(2,1)S(1)} %copy-done.14, ...), custom_call_target="tpu_custom_call" | custom-call | flops 2147483648 | bytes 12582912 | tf_op jit(solution)/shard_map/pallas_call | solution.py:160
  220.2 2.7 %shard_map.134 = f32[256,4096]{1,0:T(8,128)} custom-call(s32[4]{0:T(128)S(1)} %pad_add_fusion.1.members_ref, bf16[256,1024]{1,0:T(8,128)(2,1)S(1)} %get-tuple-element.92.refs_0_, bf16[256,1024]{1,0:T(8,128)(2,1)S(1)} %collective-permute-done.26.refs_1_, bf16[256,1024]{1,0:T(8,128)(2,1)S(1)} %collective-permute-done.27.refs_2_, ...), custom_call_target="tpu_custom_call" | custom-call | bytes 6291456 | tf_op jit(solution)/shard_map/pallas_call | solution.py:123
  222.9 2.7 %collective-permute-done.23.refs_3_ = bf16[144,1024]{1,0:T(8,128)(2,1)S(1)} collective-permute-done((bf16[144,1024]{1,0:T(8,128)(2,1)S(1)}, bf16[144,1024]{1,0:T(8,128)(2,1)S(1)}, u32[]{:S(2)}, u32[]{:S(2)}) %collective-permute-start.23) | collective-permute-done | bytes 294944 | tf_op jit(solution)/shard_map/ppermute | solution.py:29
  226.8 4.6 %collective-permute-done.22.refs_2_ = bf16[144,1024]{1,0:T(8,128)(2,1)S(1)} collective-permute-done((bf16[144,1024]{1,0:T(8,128)(2,1)S(1)}, bf16[144,1024]{1,0:T(8,128)(2,1)S(1)}, u32[]{:S(2)}, u32[]{:S(2)}) %collective-permute-start.22) | collective-permute-done | bytes 294944 | tf_op jit(solution)/shard_map/ppermute | solution.py:29
  233.5 2.8 %fusion.101 = bf16[512,1024]{1,0:T(8,128)(2,1)S(1)} fusion(bf16[512,1024]{1,0:T(8,128)(2,1)S(1)} %copy-done.26, bf16[1024,1024]{1,0:T(8,128)(2,1)} %bitcast.32), kind=kOutput, calls=%fused_computation.202 | convolution fusion | flops 1073741824 | bytes 4194304 | tf_op jit(solution)/shard_map/dot_general | solution.py:17
  237.8 3.9 %collective-permute-start.30 = (bf16[128,1024]{1,0:T(8,128)(2,1)S(1)}, bf16[128,1024]{1,0:T(8,128)(2,1)S(1)}, u32[]{:S(2)}, u32[]{:S(2)}) collective-permute-start(bf16[128,1024]{1,0:T(8,128)(2,1)S(1)} %get-tuple-element.119), channel_id=1, source_target_pairs={{0,64},{32,96},{64,0},{96,32},{1,65},{33,97},{65,1},{97,33},{2,66}... | collective-permute-start | bytes 786440 | tf_op jit(solution)/shard_map/ppermute | solution.py:29
  241.7 4.9 %collective-permute-done.31.refs_3_ = bf16[128,1024]{1,0:T(8,128)(2,1)S(1)} collective-permute-done((bf16[128,1024]{1,0:T(8,128)(2,1)S(1)}, bf16[128,1024]{1,0:T(8,128)(2,1)S(1)}, u32[]{:S(2)}, u32[]{:S(2)}) %collective-permute-start.31) | collective-permute-done | bytes 262176 | tf_op jit(solution)/shard_map/ppermute | solution.py:29
  246.5 6.3 %collective-permute-done.30.refs_2_ = bf16[128,1024]{1,0:T(8,128)(2,1)S(1)} collective-permute-done((bf16[128,1024]{1,0:T(8,128)(2,1)S(1)}, bf16[128,1024]{1,0:T(8,128)(2,1)S(1)}, u32[]{:S(2)}, u32[]{:S(2)}) %collective-permute-start.30) | collective-permute-done | bytes 262176 | tf_op jit(solution)/shard_map/ppermute | solution.py:29
  (158 shorter events, 44.3 us)
Async XLA Ops:
  2.8 16.5 %collective-permute-start = (bf16[144,1024]{1,0:T(8,128)(2,1)S(1)}, bf16[144,1024]{1,0:T(8,128)(2,1)S(1)}, u32[]{:S(2)}, u32[]{:S(2)}) collective-permute-start(bf16[144,1024]{1,0:T(8,128)(2,1)S(1)} %get-tuple-element.143), channel_id=1, source_target_pairs={{0,96},{32,0},{64,32},{96,64},{1,97},{33,1},{65,33},{97,65},{2,98}... | collective-permute-start | bytes 884744 | tf_op jit(solution)/shard_map/ppermute | solution.py:29
  5.8 13.6 %collective-permute-start.1 = (bf16[144,1024]{1,0:T(8,128)(2,1)S(1)}, bf16[144,1024]{1,0:T(8,128)(2,1)S(1)}, u32[]{:S(2)}, u32[]{:S(2)}) collective-permute-start(bf16[144,1024]{1,0:T(8,128)(2,1)S(1)} %get-tuple-element.144), channel_id=1, source_target_pairs={{0,64},{32,96},{64,0},{96,32},{1,65},{33,97},{65,1},{97,33},{2,66}... | collective-permute-start | bytes 884744 | tf_op jit(solution)/shard_map/ppermute | solution.py:29
  6.6 15.6 %collective-permute-start.2 = (bf16[144,1024]{1,0:T(8,128)(2,1)S(1)}, bf16[144,1024]{1,0:T(8,128)(2,1)S(1)}, u32[]{:S(2)}, u32[]{:S(2)}) collective-permute-start(bf16[144,1024]{1,0:T(8,128)(2,1)S(1)} %get-tuple-element.145), channel_id=1, source_target_pairs={{0,32},{32,64},{64,96},{96,0},{1,33},{33,65},{65,97},{97,1},{2,34}... | collective-permute-start | bytes 884744 | tf_op jit(solution)/shard_map/ppermute | solution.py:29
  8.3 19.4 %collective-permute-start.4 = (bf16[128,1024]{1,0:T(8,128)(2,1)}, bf16[128,1024]{1,0:T(8,128)(2,1)}, u32[]{:S(2)}, u32[]{:S(2)}) collective-permute-start(bf16[128,1024]{1,0:T(8,128)(2,1)} %get-tuple-element.131), channel_id=1, source_target_pairs={{0,32},{32,64},{64,96},{96,0},{1,33},{33,65},{65,97},{97,1},{2,34}... | collective-permute-start | bytes 786440 | tf_op jit(solution)/shard_map/ppermute | solution.py:29
  10.1 17.6 %collective-permute-start.3 = (bf16[128,1024]{1,0:T(8,128)(2,1)}, bf16[128,1024]{1,0:T(8,128)(2,1)}, u32[]{:S(2)}, u32[]{:S(2)}) collective-permute-start(bf16[128,1024]{1,0:T(8,128)(2,1)} %get-tuple-element.132), channel_id=1, source_target_pairs={{0,96},{32,0},{64,32},{96,64},{1,97},{33,1},{65,33},{97,65},{2,98}... | collective-permute-start | bytes 786440 | tf_op jit(solution)/shard_map/ppermute | solution.py:29
  27.8 37.4 %all-to-all-start = ((bf16[32,32,1024]{2,1,0:T(8,128)(2,1)}), bf16[32,32,1024]{2,1,0:T(8,128)(2,1)}, u32[]{:S(2)}, u32[]{:S(2)}) async-start(bf16[32,32,1024]{2,1,0:T(8,128)(2,1)} %bitcast.94), calls=%async_computation | async-start | bytes 4194304 | tf_op jit(solution)/shard_map/all_to_all | solution.py:413
  38.0 10.9 %collective-permute-start.5 = (bf16[128,1024]{1,0:T(8,128)(2,1)}, bf16[128,1024]{1,0:T(8,128)(2,1)S(1)}, u32[]{:S(2)}, u32[]{:S(2)}) collective-permute-start(bf16[128,1024]{1,0:T(8,128)(2,1)} %get-tuple-element.58), channel_id=1, source_target_pairs={{0,64},{32,96},{64,0},{96,32},{1,65},{33,97},{65,1},{97,33},{2,66}... | collective-permute-start | bytes 786440 | tf_op jit(solution)/shard_map/ppermute | solution.py:29
  41.4 30.9 %collective-permute-start.14 = (bf16[256,1024]{1,0:T(8,128)(2,1)}, bf16[256,1024]{1,0:T(8,128)(2,1)S(1)}, u32[]{:S(2)}, u32[]{:S(2)}) collective-permute-start(bf16[256,1024]{1,0:T(8,128)(2,1)} %get-tuple-element.63), channel_id=1, source_target_pairs={{0,64},{32,96},{64,0},{96,32},{1,65},{33,97},{65,1},{97,33},{2,66}... | collective-permute-start | bytes 1572872 | tf_op jit(solution)/shard_map/ppermute | solution.py:29
  44.1 28.2 %collective-permute-start.13 = (bf16[256,1024]{1,0:T(8,128)(2,1)}, bf16[256,1024]{1,0:T(8,128)(2,1)S(1)}, u32[]{:S(2)}, u32[]{:S(2)}) collective-permute-start(bf16[256,1024]{1,0:T(8,128)(2,1)} %get-tuple-element.62), channel_id=1, source_target_pairs={{0,96},{32,0},{64,32},{96,64},{1,97},{33,1},{65,33},{97,65},{2,98}... | collective-permute-start | bytes 1572872 | tf_op jit(solution)/shard_map/ppermute | solution.py:29
  44.7 27.6 %collective-permute-start.15 = (bf16[256,1024]{1,0:T(8,128)(2,1)}, bf16[256,1024]{1,0:T(8,128)(2,1)}, u32[]{:S(2)}, u32[]{:S(2)}) collective-permute-start(bf16[256,1024]{1,0:T(8,128)(2,1)} %get-tuple-element.64), channel_id=1, source_target_pairs={{0,32},{32,64},{64,96},{96,0},{1,33},{33,65},{65,97},{97,1},{2,34}... | collective-permute-start | bytes 1572872 | tf_op jit(solution)/shard_map/ppermute | solution.py:29
  49.0 16.2 %copy-start.27 = (bf16[512,1024]{1,0:T(8,128)(2,1)S(1)}, bf16[512,1024]{1,0:T(8,128)(2,1)}, u32[]{:S(2)}) copy-start(bf16[512,1024]{1,0:T(8,128)(2,1)} %fusion.2.place_ref) | copy-start | bytes 3145732
  69.1 26.1 %collective-permute-start.7 = (bf16[512,1024]{1,0:T(8,128)(2,1)}, bf16[512,1024]{1,0:T(8,128)(2,1)S(1)}, u32[]{:S(2)}, u32[]{:S(2)}) collective-permute-start(bf16[512,1024]{1,0:T(8,128)(2,1)} %fusion.99.refs_0_), channel_id=1, source_target_pairs={{0,32},{32,64},{64,96},{96,0},{1,33},{33,65},{65,97},{97,1},{2,34}... | collective-permute-start | bytes 3145736 | tf_op jit(solution)/shard_map/ppermute | solution.py:29
  69.1 26.3 %collective-permute-start.6 = (bf16[512,1024]{1,0:T(8,128)(2,1)}, bf16[512,1024]{1,0:T(8,128)(2,1)}, u32[]{:S(2)}, u32[]{:S(2)}) collective-permute-start(bf16[512,1024]{1,0:T(8,128)(2,1)} %fusion.99.refs_0_), channel_id=1, source_target_pairs={{0,96},{32,0},{64,32},{96,64},{1,97},{33,1},{65,33},{97,65},{2,98}... | collective-permute-start | bytes 3145736 | tf_op jit(solution)/shard_map/ppermute | solution.py:29
  73.3 44.0 %all-to-all-start.1 = ((bf16[32,32,1024]{2,1,0:T(8,128)(2,1)}), bf16[32,32,1024]{2,1,0:T(8,128)(2,1)}, u32[]{:S(2)}, u32[]{:S(2)}) async-start(bf16[32,32,1024]{2,1,0:T(8,128)(2,1)} %bitcast.98), calls=%async_computation.1 | async-start | bytes 4194304 | tf_op jit(solution)/shard_map/all_to_all | solution.py:413
  95.2 14.0 %collective-permute-start.8 = (bf16[256,1024]{1,0:T(8,128)(2,1)S(1)}, bf16[256,1024]{1,0:T(8,128)(2,1)S(1)}, u32[]{:S(2)}, u32[]{:S(2)}) collective-permute-start(bf16[256,1024]{1,0:T(8,128)(2,1)S(1)} %slice.141), channel_id=1, source_target_pairs={{0,32},{32,64},{64,96},{96,0},{1,33},{33,65},{65,97},{97,1},{2,34}... | collective-permute-start | bytes 1572872 | tf_op jit(solution)/shard_map/ppermute | solution.py:29
  96.4 13.2 %collective-permute-start.9 = (bf16[256,1024]{1,0:T(8,128)(2,1)S(1)}, bf16[256,1024]{1,0:T(8,128)(2,1)S(1)}, u32[]{:S(2)}, u32[]{:S(2)}) collective-permute-start(bf16[256,1024]{1,0:T(8,128)(2,1)S(1)} %slice.142), channel_id=1, source_target_pairs={{0,96},{32,0},{64,32},{96,64},{1,97},{33,1},{65,33},{97,65},{2,98}... | collective-permute-start | bytes 1572872 | tf_op jit(solution)/shard_map/ppermute | solution.py:29
  111.8 26.0 %copy-start.16 = (bf16[512,256]{1,0:T(8,128)(2,1)}, bf16[512,256]{1,0:T(8,128)(2,1)S(1)}, u32[]{:S(2)}) copy-start(bf16[512,256]{1,0:T(8,128)(2,1)S(1)} %get-tuple-element.87.refs_0_.refs_4_) | copy-start | bytes 786436
  111.8 13.1 %collective-permute-start.12 = (bf16[512,256]{1,0:T(8,128)(2,1)S(1)}, bf16[512,256]{1,0:T(8,128)(2,1)S(1)}, u32[]{:S(2)}, u32[]{:S(2)}) collective-permute-start(bf16[512,256]{1,0:T(8,128)(2,1)S(1)} %get-tuple-element.87.refs_0_.refs_4_), channel_id=1, source_target_pairs={{0,32},{32,64},{64,96},{96,0},{1,33},{33,65},{65,97},{97,1},{2,34}... | collective-permute-start | bytes 786440 | tf_op jit(solution)/shard_map/ppermute | solution.py:29
  112.1 18.1 %copy-start.7 = (f32[512,1]{1,0:T(8,128)}, f32[512,1]{1,0:T(8,128)S(1)}, u32[]{:S(2)}) copy-start(f32[512,1]{1,0:T(8,128)S(1)} %copy.30.refs_8_.refs_7_) | copy-start | bytes 6148
  112.1 18.0 %collective-permute-start.11 = (bf16[512,256]{1,0:T(8,128)(2,1)S(1)}, bf16[512,256]{1,0:T(8,128)(2,1)}, u32[]{:S(2)}, u32[]{:S(2)}) collective-permute-start(bf16[512,256]{1,0:T(8,128)(2,1)S(1)} %get-tuple-element.87.refs_0_.refs_4_), channel_id=1, source_target_pairs={{0,64},{32,96},{64,0},{96,32},{1,65},{33,97},{65,1},{97,33},{2,66}... | collective-permute-start | bytes 786440 | tf_op jit(solution)/shard_map/ppermute | solution.py:29
  117.3 12.9 %collective-permute-start.10 = (bf16[512,256]{1,0:T(8,128)(2,1)S(1)}, bf16[512,256]{1,0:T(8,128)(2,1)}, u32[]{:S(2)}, u32[]{:S(2)}) collective-permute-start(bf16[512,256]{1,0:T(8,128)(2,1)S(1)} %get-tuple-element.87.refs_0_.refs_4_), channel_id=1, source_target_pairs={{0,96},{32,0},{64,32},{96,64},{1,97},{33,1},{65,33},{97,65},{2,98}... | collective-permute-start | bytes 786440 | tf_op jit(solution)/shard_map/ppermute | solution.py:29
  117.3 12.9 %copy-start.5 = (bf16[1024,512]{1,0:T(8,128)(2,1)S(1)}, bf16[1024,512]{1,0:T(8,128)(2,1)}, u32[]{:S(2)}) copy-start(bf16[1024,512]{1,0:T(8,128)(2,1)} %fusion.3.refs_9_.place_ref) | copy-start | bytes 3145732
  117.3 12.9 %copy-start.15 = (bf16[256,1024]{1,0:T(8,128)(2,1)S(1)}, bf16[256,1024]{1,0:T(8,128)(2,1)}, u32[]{:S(2)}) copy-start(bf16[256,1024]{1,0:T(8,128)(2,1)} %get-tuple-element.61.refs_0_.refs_4_) | copy-start | bytes 1572868
  117.3 12.9 %copy-start.19 = (bf16[256,1024]{1,0:T(8,128)(2,1)S(1)}, bf16[256,1024]{1,0:T(8,128)(2,1)}, u32[]{:S(2)}) copy-start(bf16[256,1024]{1,0:T(8,128)(2,1)} %copy-done.18) | copy-start | bytes 1572868
  117.3 12.9 %copy-start.21 = (bf16[256,1024]{1,0:T(8,128)(2,1)S(1)}, bf16[256,1024]{1,0:T(8,128)(2,1)}, u32[]{:S(2)}) copy-start(bf16[256,1024]{1,0:T(8,128)(2,1)} %copy-done.20) | copy-start | bytes 1572868
  122.9 14.7 %collective-permute-start.18 = (bf16[512,256]{1,0:T(8,128)(2,1)S(1)}, bf16[512,256]{1,0:T(8,128)(2,1)S(1)}, u32[]{:S(2)}, u32[]{:S(2)}) collective-permute-start(bf16[512,256]{1,0:T(8,128)(2,1)S(1)} %get-tuple-element.67), channel_id=1, source_target_pairs={{0,32},{32,64},{64,96},{96,0},{1,33},{33,65},{65,97},{97,1},{2,34}... | collective-permute-start | bytes 786440 | tf_op jit(solution)/shard_map/ppermute | solution.py:29
  124.9 12.9 %collective-permute-start.17 = (bf16[512,256]{1,0:T(8,128)(2,1)S(1)}, bf16[512,256]{1,0:T(8,128)(2,1)S(1)}, u32[]{:S(2)}, u32[]{:S(2)}) collective-permute-start(bf16[512,256]{1,0:T(8,128)(2,1)S(1)} %get-tuple-element.68), channel_id=1, source_target_pairs={{0,64},{32,96},{64,0},{96,32},{1,65},{33,97},{65,1},{97,33},{2,66}... | collective-permute-start | bytes 786440 | tf_op jit(solution)/shard_map/ppermute | solution.py:29
  125.0 12.6 %copy-start.22 = (bf16[512,256]{1,0:T(8,128)(2,1)}, bf16[512,256]{1,0:T(8,128)(2,1)S(1)}, u32[]{:S(2)}) copy-start(bf16[512,256]{1,0:T(8,128)(2,1)S(1)} %collective-permute-done.12.refs_3_) | copy-start | bytes 786436
  125.0 12.6 %collective-permute-start.16 = (bf16[512,256]{1,0:T(8,128)(2,1)S(1)}, bf16[512,256]{1,0:T(8,128)(2,1)S(1)}, u32[]{:S(2)}, u32[]{:S(2)}) collective-permute-start(bf16[512,256]{1,0:T(8,128)(2,1)S(1)} %get-tuple-element.69), channel_id=1, source_target_pairs={{0,96},{32,0},{64,32},{96,64},{1,97},{33,1},{65,33},{97,65},{2,98}... | collective-permute-start | bytes 786440 | tf_op jit(solution)/shard_map/ppermute | solution.py:29
  144.2 24.8 %collective-permute-start.19 = (bf16[512,1024]{1,0:T(8,128)(2,1)}, bf16[512,1024]{1,0:T(8,128)(2,1)}, u32[]{:S(2)}, u32[]{:S(2)}) collective-permute-start(bf16[512,1024]{1,0:T(8,128)(2,1)} %get-tuple-element.78), channel_id=1, source_target_pairs={{0,32},{32,64},{64,96},{96,0},{1,33},{33,65},{65,97},{97,1},{2,34}... | collective-permute-start | bytes 3145736 | tf_op jit(solution)/shard_map/ppermute | solution.py:29
  146.2 25.4 %collective-permute-start.20 = (bf16[512,1024]{1,0:T(8,128)(2,1)}, bf16[512,1024]{1,0:T(8,128)(2,1)}, u32[]{:S(2)}, u32[]{:S(2)}) collective-permute-start(bf16[512,1024]{1,0:T(8,128)(2,1)} %get-tuple-element.79), channel_id=1, source_target_pairs={{0,96},{32,0},{64,32},{96,64},{1,97},{33,1},{65,33},{97,65},{2,98}... | collective-permute-start | bytes 3145736 | tf_op jit(solution)/shard_map/ppermute | solution.py:29
  148.3 45.4 %all-to-all-start.2 = ((bf16[32,32,1024]{2,1,0:T(8,128)(2,1)}), bf16[32,32,1024]{2,1,0:T(8,128)(2,1)}, u32[]{:S(2)}, u32[]{:S(2)}) async-start(bf16[32,32,1024]{2,1,0:T(8,128)(2,1)} %bitcast.97), calls=%async_computation.2 | async-start | bytes 4194304 | tf_op jit(solution)/shard_map/all_to_all | solution.py:413
  159.2 17.4 %copy-start.29 = (f32[512,1]{1,0:T(8,128)S(1)}, f32[512,1]{1,0:T(8,128)}, u32[]{:S(2)}) copy-start(f32[512,1]{1,0:T(8,128)} %get-tuple-element.86) | copy-start | bytes 6148
  171.2 13.9 %collective-permute-start.24 = (bf16[256,1024]{1,0:T(8,128)(2,1)}, bf16[256,1024]{1,0:T(8,128)(2,1)S(1)}, u32[]{:S(2)}, u32[]{:S(2)}) collective-permute-start(bf16[256,1024]{1,0:T(8,128)(2,1)} %add_convert_fusion.1), channel_id=1, source_target_pairs={{0,32},{32,64},{64,96},{96,0},{1,33},{33,65},{65,97},{97,1},{2,34}... | collective-permute-start | bytes 1572872 | tf_op jit(solution)/shard_map/ppermute | solution.py:29
  173.7 15.2 %collective-permute-start.25 = (bf16[256,1024]{1,0:T(8,128)(2,1)}, bf16[256,1024]{1,0:T(8,128)(2,1)}, u32[]{:S(2)}, u32[]{:S(2)}) collective-permute-start(bf16[256,1024]{1,0:T(8,128)(2,1)} %add_convert_fusion), channel_id=1, source_target_pairs={{0,96},{32,0},{64,32},{96,64},{1,97},{33,1},{65,33},{97,65},{2,98}... | collective-permute-start | bytes 1572872 | tf_op jit(solution)/shard_map/ppermute | solution.py:29
  179.6 9.3 %copy-start.4 = (f32[512,1024]{1,0:T(8,128)S(1)}, f32[512,1024]{1,0:T(8,128)}, u32[]{:S(2)}) copy-start(f32[512,1024]{1,0:T(8,128)} %convolution_add_fusion.own_ref) | copy-start | bytes 6291460
  179.6 9.3 %copy-start.6 = (bf16[1024,512]{1,0:T(8,128)(2,1)S(1)}, bf16[1024,512]{1,0:T(8,128)(2,1)}, u32[]{:S(2)}) copy-start(bf16[1024,512]{1,0:T(8,128)(2,1)} %fusion.3.refs_9_.place_ref) | copy-start | bytes 3145732
  180.8 31.3 %collective-permute-start.28 = (bf16[256,1024]{1,0:T(8,128)(2,1)}, bf16[256,1024]{1,0:T(8,128)(2,1)S(1)}, u32[]{:S(2)}, u32[]{:S(2)}) collective-permute-start(bf16[256,1024]{1,0:T(8,128)(2,1)} %get-tuple-element.110), channel_id=1, source_target_pairs={{0,32},{32,64},{64,96},{96,0},{1,33},{33,65},{65,97},{97,1},{2,34}... | collective-permute-start | bytes 1572872 | tf_op jit(solution)/shard_map/ppermute | solution.py:29
  180.8 32.3 %collective-permute-start.26 = (bf16[256,1024]{1,0:T(8,128)(2,1)}, bf16[256,1024]{1,0:T(8,128)(2,1)S(1)}, u32[]{:S(2)}, u32[]{:S(2)}) collective-permute-start(bf16[256,1024]{1,0:T(8,128)(2,1)} %get-tuple-element.112), channel_id=1, source_target_pairs={{0,96},{32,0},{64,32},{96,64},{1,97},{33,1},{65,33},{97,65},{2,98}... | collective-permute-start | bytes 1572872 | tf_op jit(solution)/shard_map/ppermute | solution.py:29
  193.8 39.8 %all-to-all-start.3 = ((bf16[32,32,1024]{2,1,0:T(8,128)(2,1)}), bf16[32,32,1024]{2,1,0:T(8,128)(2,1)}, u32[]{:S(2)}, u32[]{:S(2)}) async-start(bf16[32,32,1024]{2,1,0:T(8,128)(2,1)} %bitcast.95), calls=%async_computation.3 | async-start | bytes 4194304 | tf_op jit(solution)/shard_map/all_to_all | solution.py:413
  202.8 17.4 %collective-permute-start.27 = (bf16[256,1024]{1,0:T(8,128)(2,1)}, bf16[256,1024]{1,0:T(8,128)(2,1)S(1)}, u32[]{:S(2)}, u32[]{:S(2)}) collective-permute-start(bf16[256,1024]{1,0:T(8,128)(2,1)} %get-tuple-element.94), channel_id=1, source_target_pairs={{0,64},{32,96},{64,0},{96,32},{1,65},{33,97},{65,1},{97,33},{2,66}... | collective-permute-start | bytes 1572872 | tf_op jit(solution)/shard_map/ppermute | solution.py:29
  208.8 16.9 %collective-permute-start.23 = (bf16[144,1024]{1,0:T(8,128)(2,1)S(1)}, bf16[144,1024]{1,0:T(8,128)(2,1)S(1)}, u32[]{:S(2)}, u32[]{:S(2)}) collective-permute-start(bf16[144,1024]{1,0:T(8,128)(2,1)S(1)} %get-tuple-element.146), channel_id=1, source_target_pairs={{0,32},{32,64},{64,96},{96,0},{1,33},{33,65},{65,97},{97,1},{2,34}... | collective-permute-start | bytes 884744 | tf_op jit(solution)/shard_map/ppermute | solution.py:29
  210.9 15.8 %collective-permute-start.21 = (bf16[144,1024]{1,0:T(8,128)(2,1)S(1)}, bf16[144,1024]{1,0:T(8,128)(2,1)S(1)}, u32[]{:S(2)}, u32[]{:S(2)}) collective-permute-start(bf16[144,1024]{1,0:T(8,128)(2,1)S(1)} %get-tuple-element.147), channel_id=1, source_target_pairs={{0,96},{32,0},{64,32},{96,64},{1,97},{33,1},{65,33},{97,65},{2,98}... | collective-permute-start | bytes 884744 | tf_op jit(solution)/shard_map/ppermute | solution.py:29
  212.1 19.2 %collective-permute-start.22 = (bf16[144,1024]{1,0:T(8,128)(2,1)S(1)}, bf16[144,1024]{1,0:T(8,128)(2,1)S(1)}, u32[]{:S(2)}, u32[]{:S(2)}) collective-permute-start(bf16[144,1024]{1,0:T(8,128)(2,1)S(1)} %get-tuple-element.148), channel_id=1, source_target_pairs={{0,64},{32,96},{64,0},{96,32},{1,65},{33,97},{65,1},{97,33},{2,66}... | collective-permute-start | bytes 884744 | tf_op jit(solution)/shard_map/ppermute | solution.py:29
  222.9 10.6 %copy-start.26 = (bf16[512,1024]{1,0:T(8,128)(2,1)S(1)}, bf16[512,1024]{1,0:T(8,128)(2,1)}, u32[]{:S(2)}) copy-start(bf16[512,1024]{1,0:T(8,128)(2,1)} %fusion.1) | copy-start | bytes 3145732
  236.4 10.1 %collective-permute-start.31 = (bf16[128,1024]{1,0:T(8,128)(2,1)S(1)}, bf16[128,1024]{1,0:T(8,128)(2,1)S(1)}, u32[]{:S(2)}, u32[]{:S(2)}) collective-permute-start(bf16[128,1024]{1,0:T(8,128)(2,1)S(1)} %get-tuple-element.118), channel_id=1, source_target_pairs={{0,32},{32,64},{64,96},{96,0},{1,33},{33,65},{65,97},{97,1},{2,34}... | collective-permute-start | bytes 786440 | tf_op jit(solution)/shard_map/ppermute | solution.py:29
  237.8 15.0 %collective-permute-start.30 = (bf16[128,1024]{1,0:T(8,128)(2,1)S(1)}, bf16[128,1024]{1,0:T(8,128)(2,1)S(1)}, u32[]{:S(2)}, u32[]{:S(2)}) collective-permute-start(bf16[128,1024]{1,0:T(8,128)(2,1)S(1)} %get-tuple-element.119), channel_id=1, source_target_pairs={{0,64},{32,96},{64,0},{96,32},{1,65},{33,97},{65,1},{97,33},{2,66}... | collective-permute-start | bytes 786440 | tf_op jit(solution)/shard_map/ppermute | solution.py:29
  241.7 11.2 %collective-permute-start.29 = (bf16[128,1024]{1,0:T(8,128)(2,1)S(1)}, bf16[128,1024]{1,0:T(8,128)(2,1)S(1)}, u32[]{:S(2)}, u32[]{:S(2)}) collective-permute-start(bf16[128,1024]{1,0:T(8,128)(2,1)S(1)} %get-tuple-element.120), channel_id=1, source_target_pairs={{0,96},{32,0},{64,32},{96,64},{1,97},{33,1},{65,33},{97,65},{2,98}... | collective-permute-start | bytes 786440 | tf_op jit(solution)/shard_map/ppermute | solution.py:29
  (19 other events, 76.7 us)
where the time goes:
time: 255 us; the launch traced here: 254 us
  starting transfers between devices  82.2 us (32%)
  waiting for transfers between devices  79.9 us (31%)
  Pallas kernels  42.2 us (17%)
  matrix products  31.3 us (12%)
  other arithmetic  8.89 us (3%)
  local copies, waits for them, and re-layouts  8.57 us (3%)
    ppermute x32, waiting for transfers between devices, shift(): lax.ppermute(value, 'pool', [(i, (i + step) % size) for i in range(size)])  67.4 us
    ppermute x32, starting transfers between devices, shift(): lax.ppermute(value, 'pool', [(i, (i + step) % size) for i in range(size)])  52.6 us
    dot_general x17, matrix products, dot(): return lax.dot_general(a, b, (dims, ((), ())), preferred_element_type=out)  31.3 us
    all_to_all x4, starting transfers between devices, exchange(): lax.all_to_all(blocks, 'ep', split_axis=0, concat_axis=0, tiled=True)  29.6 us
    all_to_all x4, waiting for transfers between devices, exchange(): lax.all_to_all(blocks, 'ep', split_axis=0, concat_axis=0, tiled=True)  12.5 us
    pallas_call x1, Pallas kernels, weighted_slots(): pl.pallas_call(kernel, grid=(4,), in_specs=[whole_block((count, share))]...  7.3 us
    pallas_call x1, Pallas kernels, weight_grads(): pl.pallas_call(kernel, grid_spec=pltpu.PrefetchScalarGridSpec(num_scalar_...  7.09 us
    pallas_call x1, Pallas kernels, first_hop(): pl.pallas_call(kernel, grid_spec=pltpu.PrefetchScalarGridSpec(num_scalar_...  6.34 us
  transfers between devices with their start and end apart: 36, of which 19 were waited for; matrix products, arithmetic and copies ran while one was open for 16% of the time, Pallas kernels for 13%

commit v1 on v0

--- a/solution.py
+++ b/solution.py
@@ -73,6 +73,33 @@
 def cost(flops, arrays):
     size = sum(int(array.size) * jnp.dtype(array.dtype).itemsize for array in arrays)
     return pl.CostEstimate(flops=int(flops), bytes_accessed=size, transcendentals=0)
+
+
+def token_messages(tokens, modality, members):
+    rows, width = tokens.shape
+    cols = width // members.shape[0]
+
+    def kernel(members_ref, tokens_ref, modality_ref, *outs):
+        for d, out in enumerate(outs):
+            start = pl.multiple_of(members_ref[d] * cols, 128)
+            out[:rows, :] = tokens_ref[:, pl.ds(start, cols)]
+            out[rows:, :] = jnp.zeros((16, cols), BF16)
+            kinds = jnp.broadcast_to(modality_ref[...].astype(F32), (16, rows))
+            out[rows:, :rows] = kinds.astype(BF16)
+
+    message = jax.ShapeDtypeStruct((rows + 16, cols), BF16)
+    return pl.pallas_call(
+        kernel,
+        grid_spec=pltpu.PrefetchScalarGridSpec(
+            num_scalar_prefetch=1,
+            grid=(1,),
+            in_specs=[whole_block((rows, width)), whole_block((1, rows))],
+            out_specs=[whole_block(message.shape)] * members.shape[0],
+        ),
+        out_shape=[message] * members.shape[0],
+        cost_estimate=cost(0, (tokens, tokens)),
+        compiler_params=params(8),
+    )(members, tokens, modality.reshape(1, rows))
 
 
 def masked_send(pick, parts, text_rows):
@@ -173,6 +200,25 @@
         ),
         compiler_params=params(16),
     )(members, *pieces, gate_back, up_back)
+
+
+def fetch_rows(place_in, got):
+    count, total = place_in.shape
+    cols = got.shape[1]
+    tile = cols // 4
+
+    def kernel(place_ref, got_ref, out_ref):
+        out_ref[...] = dot(place_ref[...], got_ref[...], ROW_COL).astype(BF16)
+
+    return pl.pallas_call(
+        kernel,
+        grid=(4,),
+        in_specs=[whole_block((count, total)), pl.BlockSpec((total, tile), lambda i: (0, i))],
+        out_specs=pl.BlockSpec((count, tile), lambda i: (0, i)),
+        out_shape=kept((count, cols), BF16),
+        cost_estimate=cost(2 * count * total * cols, (place_in, got, place_in)),
+        compiler_params=params(8),
+    )(place_in, got)
 
 
 def hidden_from(gate_sum, up_sum, far, w_gate, w_up, members):
@@ -373,8 +419,9 @@
             array, (members[d % size] * count, 0), (count, array.shape[1])
         )
 
-    extra = jnp.broadcast_to(jnp.pad(modality, (0, cols - tok_rows)).astype(BF16), (16, cols))
-    token_parts = swap(lambda d: jnp.concatenate([columns(tokens)(d), extra], axis=0))
+    messages = token_messages(tokens, modality, pool_order)
+    token_parts = swap(lambda d: messages[d % size])
+    cotangent = after(cotangent, *messages)
     later = token_parts[1:]
     grad_parts = swap(lambda d: after(columns(cotangent)(d), *later) if d == 2 else columns(cotangent)(d))
     down_parts = swap(lambda d: after(columns(w_down[0])(d), *later))
@@ -413,9 +460,6 @@
         blocks = lax.all_to_all(blocks, "ep", split_axis=0, concat_axis=0, tiled=True)
         return blocks.reshape(slot_total, cols)
 
-    def fetch(got):
-        return dot(place_in, got, ROW_COL, BF16)
-
     def collect(got):
         return dot(pick_back, got, ROW_COL, BF16)
 
@@ -426,7 +470,7 @@
     weight = gates[0][:, None]
     sent = masked_send(pick, token_parts, text_count * size * slots)
     sent_grads = dot(pick, jnp.concatenate(grad_parts, axis=0), ROW_COL, BF16)
-    block = fetch(after(exchange(after(sent, grad_parts[1], grad_parts[3])), sent_grads))
+    block = fetch_rows(place_in, after(exchange(sent), sent_grads))
     inputs = ring_gather(block)
     got = exchange(after(sent_grads, block, *down_parts))
 
@@ -454,9 +498,10 @@
         return dot(gate, rows(wg, cols)(d), COL_COL) + dot(up, rows(wu, cols)(d), COL_COL)
 
     own = share_in(0, slice(None))
+    behind = lax.optimization_barrier(share_in(3, slice(half, None)))
     hops = (
         (share_in(1, slice(0, half)) + rise[:half].astype(F32)).astype(BF16),
-        (share_in(3, slice(half, None)) + fall[half:].astype(F32)).astype(BF16),
+        add(behind, fall[half:]).astype(BF16),
     )
     last = shift(hops[0], 1), shift(hops[1], -1)
     slots_in = summed_slots(own, rise, fall, *last, place_out)

time: 255 us -> 255 us (level)
  matrix products: 31.3 us -> 25.3 us
  waiting for transfers between devices: 79.9 us -> 76.1 us
  Pallas kernels: 42.2 us -> 45.7 us
  other arithmetic: 8.89 us -> 11.7 us
    all_to_all x4, waiting for transfers between devices: 12.5 us -> 0.01 us  [exchange(): lax.all_to_all(blocks, 'ep', split_axis=0, concat_axis=0, tiled=True)]
    ppermute x32, waiting for transfers between devices: 67.4 us -> 76.1 us  [shift(): lax.ppermute(value, 'pool', [(i, (i + step) % size) for i in range(size)])]
    dot_general x17 -> x16, matrix products: 31.3 us -> 25.3 us  [dot(): return lax.dot_general(a, b, (dims, ((), ())), preferred_element_type=out)]
    pallas_call x0 -> x2, Pallas kernels: none -> 3.6 us  [the longest x1 2.99 us: fetch_rows(): pl.pallas_call(kernel, grid=(4,), in_specs=[whole_block((count, total)),...]
  transfers between devices with their start and end apart: 36 -> 36, of which waited for: 19 -> 18; matrix products, arithmetic and copies ran while one was open for 16% -> 16% of each run, Pallas kernels for 13% -> 13%
where the time goes in v1:
time: 255 us; the launch traced here: 254 us
  starting transfers between devices  83.1 us (33%)
  waiting for transfers between devices  76.1 us (30%)
  Pallas kernels  45.7 us (18%)
  matrix products  25.3 us (10%)
  other arithmetic  11.7 us (5%)
  local copies, waits for them, and re-layouts  10.4 us (4%)
    ppermute x32, waiting for transfers between devices, shift(): lax.ppermute(value, 'pool', [(i, (i + step) % size) for i in range(size)])  76.1 us
    ppermute x32, starting transfers between devices, shift(): lax.ppermute(value, 'pool', [(i, (i + step) % size) for i in range(size)])  52.1 us
    all_to_all x4, starting transfers between devices, exchange(): lax.all_to_all(blocks, 'ep', split_axis=0, concat_axis=0, tiled=True)  31 us
    dot_general x16, matrix products, dot(): return lax.dot_general(a, b, (dims, ((), ())), preferred_element_type=out)  25.3 us
    pallas_call x1, Pallas kernels, weighted_slots(): pl.pallas_call(kernel, grid=(4,), in_specs=[whole_block((count, share))]...  7.17 us
    pallas_call x1, Pallas kernels, weight_grads(): pl.pallas_call(kernel, grid_spec=pltpu.PrefetchScalarGridSpec(num_scalar_...  7.1 us
    pallas_call x1, Pallas kernels, first_hop(): pl.pallas_call(kernel, grid_spec=pltpu.PrefetchScalarGridSpec(num_scalar_...  6.37 us
    pallas_call x3, Pallas kernels, assemble(): pl.pallas_call(kernel, grid_spec=pltpu.PrefetchScalarGridSpec(num_scalar_...  5.85 us
  transfers between devices with their start and end apart: 36, of which 18 were waited for; matrix products, arithmetic and copies ran while one was open for 16% of the time, Pallas kernels for 13%

profile of v1, /device:TPU:0, one launch (start us, length us, event | category | flops | bytes accessed | tf_op | source)
XLA Modules:
  0.0 253.6 jit_solution(16980601508245613592)
XLA Ops:
  3.3 2.9 %collective-permute-start = (bf16[144,1024]{1,0:T(8,128)(2,1)S(1)}, bf16[144,1024]{1,0:T(8,128)(2,1)S(1)}, u32[]{:S(2)}, u32[]{:S(2)}) collective-permute-start(bf16[144,1024]{1,0:T(8,128)(2,1)S(1)} %get-tuple-element.62), channel_id=1, source_target_pairs={{0,96},{32,0},{64,32},{96,64},{1,97},{33,1},{65,33},{97,65},{2,98}... | collective-permute-start | bytes 884744 | tf_op jit(solution)/shard_map/ppermute | solution.py:29
  14.0 4.8 %collective-permute-done.refs_1_ = bf16[144,1024]{1,0:T(8,128)(2,1)S(1)} collective-permute-done((bf16[144,1024]{1,0:T(8,128)(2,1)S(1)}, bf16[144,1024]{1,0:T(8,128)(2,1)S(1)}, u32[]{:S(2)}, u32[]{:S(2)}) %collective-permute-start) | collective-permute-done | bytes 294944 | tf_op jit(solution)/shard_map/ppermute | solution.py:29
  18.8 3.7 %collective-permute-done.2.refs_3_ = bf16[144,1024]{1,0:T(8,128)(2,1)S(1)} collective-permute-done((bf16[144,1024]{1,0:T(8,128)(2,1)S(1)}, bf16[144,1024]{1,0:T(8,128)(2,1)S(1)}, u32[]{:S(2)}, u32[]{:S(2)}) %collective-permute-start.2) | collective-permute-done | bytes 294944 | tf_op jit(solution)/shard_map/ppermute | solution.py:29
  22.5 3.1 %shard_map.128 = bf16[1024,1024]{1,0:T(8,128)(2,1)} custom-call(bf16[1024,512]{1,0:T(8,128)(2,1)S(1)} %fusion.pick_ref, bf16[144,1024]{1,0:T(8,128)(2,1)S(1)} %get-tuple-element.61.refs_0_, bf16[144,1024]{1,0:T(8,128)(2,1)S(1)} %collective-permute-done.refs_1_, bf16[144,1024]{1,0:T(8,128)(2,1)S(1)} %collective-permute-done.1.refs_2_, ...), custom_call_target="tpu_custom_call" | custom-call | flops 1073741824 | bytes 5242880 | tf_op jit(solution)/shard_map/pallas_call | solution.py:127
  25.5 8.5 %all-to-all-start = ((bf16[32,32,1024]{2,1,0:T(8,128)(2,1)}), bf16[32,32,1024]{2,1,0:T(8,128)(2,1)S(1)}, u32[]{:S(2)}, u32[]{:S(2)}) async-start(bf16[32,32,1024]{2,1,0:T(8,128)(2,1)} %bitcast.93), calls=%async_computation | async-start | bytes 4194304 | tf_op jit(solution)/shard_map/all_to_all | solution.py:460
  34.9 3.2 %collective-permute-start.3 = (bf16[128,1024]{1,0:T(8,128)(2,1)}, bf16[128,1024]{1,0:T(8,128)(2,1)}, u32[]{:S(2)}, u32[]{:S(2)}) collective-permute-start(bf16[128,1024]{1,0:T(8,128)(2,1)} %get-tuple-element.137), channel_id=1, source_target_pairs={{0,96},{32,0},{64,32},{96,64},{1,97},{33,1},{65,33},{97,65},{2,98}... | collective-permute-start | bytes 786440 | tf_op jit(solution)/shard_map/ppermute | solution.py:29
  42.5 3.5 %collective-permute-start.14 = (bf16[256,1024]{1,0:T(8,128)(2,1)}, bf16[256,1024]{1,0:T(8,128)(2,1)}, u32[]{:S(2)}, u32[]{:S(2)}) collective-permute-start(bf16[256,1024]{1,0:T(8,128)(2,1)} %get-tuple-element.71), channel_id=1, source_target_pairs={{0,64},{32,96},{64,0},{96,32},{1,65},{33,97},{65,1},{97,33},{2,66}... | collective-permute-start | bytes 1572872 | tf_op jit(solution)/shard_map/ppermute | solution.py:29
  46.0 2.0 collective-permute-start.15
  48.0 14.0 %collective-permute-done.3 = bf16[128,1024]{1,0:T(8,128)(2,1)} collective-permute-done((bf16[128,1024]{1,0:T(8,128)(2,1)}, bf16[128,1024]{1,0:T(8,128)(2,1)}, u32[]{:S(2)}, u32[]{:S(2)}) %collective-permute-start.3) | collective-permute-done | bytes 262176 | tf_op jit(solution)/shard_map/ppermute | solution.py:29
  62.0 3.6 %fusion.5 = bf16[1024,1024]{1,0:T(8,128)(2,1)} fusion(bf16[1024,512]{1,0:T(8,128)(2,1)S(1)} %copy-done.8, bf16[128,1024]{1,0:T(8,128)(2,1)} %collective-permute-done.5, bf16[128,1024]{1,0:T(8,128)(2,1)S(1)} %collective-permute-done.4, bf16[128,1024]{1,0:T(8,128)(2,1)} %collective-permute-done.3, bf16[128,1024]{1,0:T(8,128)(2,1)S(1)} %get-tuple-element.134), kind=kOutput, calls=%fused_computation.17 | convolution fusion | flops 1077936128 | bytes 4194304 | tf_op jit(solution)/shard_map/dot_general | solution.py:17
  65.6 3.0 %shard_map.129.refs_0_ = bf16[512,1024]{1,0:T(8,128)(2,1)} custom-call(bf16[512,1024]{1,0:T(8,128)(2,1)S(1)} %fusion.2.place_ref, bf16[1024,1024]{1,0:T(8,128)(2,1)S(1)} %bitcast.91), custom_call_target="tpu_custom_call" | custom-call | flops 1073741824 | bytes 4194304 | tf_op jit(solution)/shard_map/pallas_call | solution.py:213
  68.6 3.7 %collective-permute-start.6 = (bf16[512,1024]{1,0:T(8,128)(2,1)}, bf16[512,1024]{1,0:T(8,128)(2,1)}, u32[]{:S(2)}, u32[]{:S(2)}) collective-permute-start(bf16[512,1024]{1,0:T(8,128)(2,1)} %shard_map.129.refs_0_), channel_id=1, source_target_pairs={{0,96},{32,0},{64,32},{96,64},{1,97},{33,1},{65,33},{97,65},{2,98}... | collective-permute-start | bytes 3145736 | tf_op jit(solution)/shard_map/ppermute | solution.py:29
  73.3 8.0 %all-to-all-start.1 = ((bf16[32,32,1024]{2,1,0:T(8,128)(2,1)}), bf16[32,32,1024]{2,1,0:T(8,128)(2,1)}, u32[]{:S(2)}, u32[]{:S(2)}) async-start(bf16[32,32,1024]{2,1,0:T(8,128)(2,1)} %bitcast.97), calls=%async_computation.1 | async-start | bytes 4194304 | tf_op jit(solution)/shard_map/all_to_all | solution.py:460
  83.3 12.2 %collective-permute-done.7.refs_4_ = bf16[512,1024]{1,0:T(8,128)(2,1)} collective-permute-done((bf16[512,1024]{1,0:T(8,128)(2,1)}, bf16[512,1024]{1,0:T(8,128)(2,1)}, u32[]{:S(2)}, u32[]{:S(2)}) %collective-permute-start.7) | collective-permute-done | bytes 1048608 | tf_op jit(solution)/shard_map/ppermute | solution.py:29
  97.8 3.3 %collective-permute-start.9 = (bf16[256,1024]{1,0:T(8,128)(2,1)S(1)}, bf16[256,1024]{1,0:T(8,128)(2,1)S(1)}, u32[]{:S(2)}, u32[]{:S(2)}) collective-permute-start(bf16[256,1024]{1,0:T(8,128)(2,1)S(1)} %slice.142), channel_id=1, source_target_pairs={{0,96},{32,0},{64,32},{96,64},{1,97},{33,1},{65,33},{97,65},{2,98}... | collective-permute-start | bytes 1572872 | tf_op jit(solution)/shard_map/ppermute | solution.py:29
  107.8 2.8 %collective-permute-done.8.top.refs_2_ = bf16[256,1024]{1,0:T(8,128)(2,1)S(1)} collective-permute-done((bf16[256,1024]{1,0:T(8,128)(2,1)S(1)}, bf16[256,1024]{1,0:T(8,128)(2,1)S(1)}, u32[]{:S(2)}, u32[]{:S(2)}) %collective-permute-start.8) | collective-permute-done | bytes 524320 | tf_op jit(solution)/shard_map/ppermute | solution.py:29
  111.0 2.2 shard_map.130
  114.4 4.3 %collective-permute-start.11 = (bf16[512,256]{1,0:T(8,128)(2,1)S(1)}, bf16[512,256]{1,0:T(8,128)(2,1)S(1)}, u32[]{:S(2)}, u32[]{:S(2)}) collective-permute-start(bf16[512,256]{1,0:T(8,128)(2,1)S(1)} %get-tuple-element.95.refs_0_.refs_4_), channel_id=1, source_target_pairs={{0,64},{32,96},{64,0},{96,32},{1,65},{33,97},{65,1},{97,33},{2,66}... | collective-permute-start | bytes 786440 | tf_op jit(solution)/shard_map/ppermute | solution.py:29
  118.7 5.5 %shard_map.131 = (bf16[512,1024]{1,0:T(8,128)(2,1)}, f32[512,256]{1,0:T(8,128)S(1)}, bf16[512,256]{1,0:T(8,128)(2,1)S(1)}, bf16[512,256]{1,0:T(8,128)(2,1)S(1)}, bf16[512,256]{1,0:T(8,128)(2,1)S(1)}) custom-call(bf16[512,1024]{1,0:T(8,128)(2,1)} %copy-done.6, bf16[1024,1024]{1,0:T(8,128)(2,1)} %bitcast.28.got_ref, ...), custom_call_target="tpu_custom_call" | custom-call | flops 2147483648 | bytes 5242880 | tf_op jit(solution)/shard_map/pallas_call | solution.py:267
  124.2 2.0 collective-permute-start.18
  126.3 2.6 %collective-permute-start.16 = (bf16[512,256]{1,0:T(8,128)(2,1)S(1)}, bf16[512,256]{1,0:T(8,128)(2,1)S(1)}, u32[]{:S(2)}, u32[]{:S(2)}) collective-permute-start(bf16[512,256]{1,0:T(8,128)(2,1)S(1)} %get-tuple-element.77), channel_id=1, source_target_pairs={{0,96},{32,0},{64,32},{96,64},{1,97},{33,1},{65,33},{97,65},{2,98}... | collective-permute-start | bytes 786440 | tf_op jit(solution)/shard_map/ppermute | solution.py:29
  129.0 2.4 collective-permute-done.11.refs_2_
  131.7 7.2 %shard_map.132 = bf16[1024,1024]{1,0:T(8,128)(2,1)} custom-call(bf16[512,256]{1,0:T(8,128)(2,1)S(1)} %get-tuple-element.95.refs_0_.refs_4_, bf16[512,256]{1,0:T(8,128)(2,1)S(1)} %collective-permute-done.10.refs_1_, bf16[512,256]{1,0:T(8,128)(2,1)S(1)} %collective-permute-done.11.refs_2_, bf16[512,256]{1,0:T(8,128)(2,1)S(1)} %collective-permute-done.12.refs_3_, ...), custom_call_target="tpu_custom_call" | custom-call | flops 2147483648 | bytes 5242880 | tf_op jit(solution)/shard_map/pallas_call | solution.py:294
  139.2 6.4 %shard_map.133 = (bf16[512,256]{1,0:T(8,128)(2,1)}, bf16[512,256]{1,0:T(8,128)(2,1)}, bf16[512,1024]{1,0:T(8,128)(2,1)}, bf16[512,1024]{1,0:T(8,128)(2,1)}, f32[512,1]{1,0:T(8,128)}) custom-call(s32[3]{0:T(128)S(1)} %pad_add_fusion.2.order_ref, f32[512,256]{1,0:T(8,128)S(1)} %get-tuple-element.74.refs_0_, ...), custom_call_target="tpu_custom_call" | custom-call | flops 1073741824 | bytes 6553600 | tf_op jit(solution)/shard_map/pallas_call | solution.py:351
  145.6 1.8 collective-permute-start.19
  147.4 2.1 collective-permute-start.20
  149.6 7.4 %all-to-all-start.2 = ((bf16[32,32,1024]{2,1,0:T(8,128)(2,1)}), bf16[32,32,1024]{2,1,0:T(8,128)(2,1)}, u32[]{:S(2)}, u32[]{:S(2)}) async-start(bf16[32,32,1024]{2,1,0:T(8,128)(2,1)} %bitcast.96), calls=%async_computation.2 | async-start | bytes 4194304 | tf_op jit(solution)/shard_map/all_to_all | solution.py:460
  161.4 9.1 %collective-permute-done.19.rise_ref = bf16[512,1024]{1,0:T(8,128)(2,1)} collective-permute-done((bf16[512,1024]{1,0:T(8,128)(2,1)}, bf16[512,1024]{1,0:T(8,128)(2,1)}, u32[]{:S(2)}, u32[]{:S(2)}) %collective-permute-start.19) | collective-permute-done | bytes 1048608 | tf_op jit(solution)/shard_map/ppermute | solution.py:29
  170.5 2.2 add_convert_fusion.1
  173.1 2.0 add_convert_fusion
  175.1 2.9 %collective-permute-start.25 = (bf16[256,1024]{1,0:T(8,128)(2,1)}, bf16[256,1024]{1,0:T(8,128)(2,1)}, u32[]{:S(2)}, u32[]{:S(2)}) collective-permute-start(bf16[256,1024]{1,0:T(8,128)(2,1)} %add_convert_fusion), channel_id=1, source_target_pairs={{0,96},{32,0},{64,32},{96,64},{1,97},{33,1},{65,33},{97,65},{2,98}... | collective-permute-start | bytes 1572872 | tf_op jit(solution)/shard_map/ppermute | solution.py:29
  178.2 2.6 %fusion.4 = bf16[1024,1024]{1,0:T(8,128)(2,1)S(1)} fusion(bf16[512,1024]{1,0:T(8,128)(2,1)} %get-tuple-element.99, bf16[512,256]{1,0:T(8,128)(2,1)S(1)} %copy-done.25, bf16[512,256]{1,0:T(8,128)(2,1)S(1)} %copy-done.27, bf16[512,256]{1,0:T(8,128)(2,1)S(1)} %copy-done.29, bf16[512,256]{1,0:T(8,128)(2,1)S(1)} %copy-done.22, f32[512]{0:T(512)S(1)} %bitcast.107), kind=kOutput, calls=%fused_computation.16 | convolution fusion | flops 1078984704 | bytes 4196352 | tf_op jit(solution)/shard_map/dot_general | solution.py:17
  182.0 3.2 %collective-permute-start.26 = (bf16[256,1024]{1,0:T(8,128)(2,1)}, bf16[256,1024]{1,0:T(8,128)(2,1)S(1)}, u32[]{:S(2)}, u32[]{:S(2)}) collective-permute-start(bf16[256,1024]{1,0:T(8,128)(2,1)} %get-tuple-element.120), channel_id=1, source_target_pairs={{0,96},{32,0},{64,32},{96,64},{1,97},{33,1},{65,33},{97,65},{2,98}... | collective-permute-start | bytes 1572872 | tf_op jit(solution)/shard_map/ppermute | solution.py:29
  185.2 1.9 collective-permute-done.24.rise_last_ref
  187.1 3.4 %collective-permute-done.25.fall_last_ref = bf16[256,1024]{1,0:T(8,128)(2,1)} collective-permute-done((bf16[256,1024]{1,0:T(8,128)(2,1)}, bf16[256,1024]{1,0:T(8,128)(2,1)}, u32[]{:S(2)}, u32[]{:S(2)}) %collective-permute-start.25) | collective-permute-done | bytes 524320 | tf_op jit(solution)/shard_map/ppermute | solution.py:29
  190.5 4.8 %shard_map.135 = bf16[1024,1024]{1,0:T(8,128)(2,1)} custom-call(f32[512,1024]{1,0:T(8,128)S(1)} %copy-done.5, bf16[512,1024]{1,0:T(8,128)(2,1)} %collective-permute-done.19.rise_ref, bf16[512,1024]{1,0:T(8,128)(2,1)} %collective-permute-done.20.fall_ref, bf16[256,1024]{1,0:T(8,128)(2,1)S(1)} %collective-permute-done.24.rise_last_ref, ...), custom_call_target="tpu_custom_call" | custom-call | flops 1073741824 | bytes 6291456 | tf_op jit(solution)/shard_map/pallas_call | solution.py:380
  195.4 7.2 %all-to-all-start.3 = ((bf16[32,32,1024]{2,1,0:T(8,128)(2,1)}), bf16[32,32,1024]{2,1,0:T(8,128)(2,1)}, u32[]{:S(2)}, u32[]{:S(2)}) async-start(bf16[32,32,1024]{2,1,0:T(8,128)(2,1)} %bitcast.94), calls=%async_computation.3 | async-start | bytes 4194304 | tf_op jit(solution)/shard_map/all_to_all | solution.py:460
  202.6 1.9 collective-permute-start.27
  204.5 3.2 %fusion.97 = bf16[512,1024]{1,0:T(8,128)(2,1)S(1)} fusion(bf16[512,1024]{1,0:T(8,128)(2,1)} %fusion.1, bf16[1024,1024]{1,0:T(8,128)(2,1)} %bitcast.31), kind=kOutput, calls=%fused_computation.192 | convolution fusion | flops 1073741824 | bytes 4194304 | tf_op jit(solution)/shard_map/dot_general | solution.py:17
  207.9 2.4 collective-permute-start.23
  212.5 7.1 %shard_map.137 = (f32[4096,256]{1,0:T(8,128)}, f32[4096,256]{1,0:T(8,128)}) custom-call(s32[4]{0:T(128)S(1)} %pad_add_fusion.1.members_ref, bf16[512,1024]{1,0:T(8,128)(2,1)S(1)} %copy-done.4, bf16[512,1024]{1,0:T(8,128)(2,1)} %collective-permute-done.6.refs_1_, bf16[256,1024]{1,0:T(8,128)(2,1)S(1)} %copy-done.17, bf16[256,1024]{1,0:T(8,128)(2,1)S(1)} %copy-done.19, ...), custom_call_target="tpu_custom_call" | custom-call | flops 2147483648 | bytes 12582912 | tf_op jit(solution)/shard_map/pallas_call | solution.py:187
  219.6 2.7 %shard_map.136 = f32[256,4096]{1,0:T(8,128)} custom-call(s32[4]{0:T(128)S(1)} %pad_add_fusion.1.members_ref, bf16[256,1024]{1,0:T(8,128)(2,1)S(1)} %get-tuple-element.100.refs_0_, bf16[256,1024]{1,0:T(8,128)(2,1)S(1)} %collective-permute-done.26.refs_1_, bf16[256,1024]{1,0:T(8,128)(2,1)S(1)} %collective-permute-done.27.refs_2_, ...), custom_call_target="tpu_custom_call" | custom-call | bytes 6291456 | tf_op jit(solution)/shard_map/pallas_call | solution.py:150
  222.3 3.0 %collective-permute-done.23.refs_3_ = bf16[144,1024]{1,0:T(8,128)(2,1)S(1)} collective-permute-done((bf16[144,1024]{1,0:T(8,128)(2,1)S(1)}, bf16[144,1024]{1,0:T(8,128)(2,1)S(1)}, u32[]{:S(2)}, u32[]{:S(2)}) %collective-permute-start.23) | collective-permute-done | bytes 294944 | tf_op jit(solution)/shard_map/ppermute | solution.py:29
  226.0 5.0 %collective-permute-done.22.refs_2_ = bf16[144,1024]{1,0:T(8,128)(2,1)S(1)} collective-permute-done((bf16[144,1024]{1,0:T(8,128)(2,1)S(1)}, bf16[144,1024]{1,0:T(8,128)(2,1)S(1)}, u32[]{:S(2)}, u32[]{:S(2)}) %collective-permute-start.22) | collective-permute-done | bytes 294944 | tf_op jit(solution)/shard_map/ppermute | solution.py:29
  233.1 2.9 %fusion.98 = bf16[512,1024]{1,0:T(8,128)(2,1)S(1)} fusion(bf16[512,1024]{1,0:T(8,128)(2,1)S(1)} %copy-done.32, bf16[1024,1024]{1,0:T(8,128)(2,1)} %bitcast.33), kind=kOutput, calls=%fused_computation.193 | convolution fusion | flops 1073741824 | bytes 4194304 | tf_op jit(solution)/shard_map/dot_general | solution.py:17
  237.0 3.9 %collective-permute-start.30 = (bf16[128,1024]{1,0:T(8,128)(2,1)S(1)}, bf16[128,1024]{1,0:T(8,128)(2,1)S(1)}, u32[]{:S(2)}, u32[]{:S(2)}) collective-permute-start(bf16[128,1024]{1,0:T(8,128)(2,1)S(1)} %get-tuple-element.127), channel_id=1, source_target_pairs={{0,64},{32,96},{64,0},{96,32},{1,65},{33,97},{65,1},{97,33},{2,66}... | collective-permute-start | bytes 786440 | tf_op jit(solution)/shard_map/ppermute | solution.py:29
  240.9 4.9 %collective-permute-done.31.refs_3_ = bf16[128,1024]{1,0:T(8,128)(2,1)S(1)} collective-permute-done((bf16[128,1024]{1,0:T(8,128)(2,1)S(1)}, bf16[128,1024]{1,0:T(8,128)(2,1)S(1)}, u32[]{:S(2)}, u32[]{:S(2)}) %collective-permute-start.31) | collective-permute-done | bytes 262176 | tf_op jit(solution)/shard_map/ppermute | solution.py:29
  245.8 6.3 %collective-permute-done.30.refs_2_ = bf16[128,1024]{1,0:T(8,128)(2,1)S(1)} collective-permute-done((bf16[128,1024]{1,0:T(8,128)(2,1)S(1)}, bf16[128,1024]{1,0:T(8,128)(2,1)S(1)}, u32[]{:S(2)}, u32[]{:S(2)}) %collective-permute-start.30) | collective-permute-done | bytes 262176 | tf_op jit(solution)/shard_map/ppermute | solution.py:29
  (165 shorter events, 43.7 us)
Async XLA Ops:
  3.3 15.5 %collective-permute-start = (bf16[144,1024]{1,0:T(8,128)(2,1)S(1)}, bf16[144,1024]{1,0:T(8,128)(2,1)S(1)}, u32[]{:S(2)}, u32[]{:S(2)}) collective-permute-start(bf16[144,1024]{1,0:T(8,128)(2,1)S(1)} %get-tuple-element.62), channel_id=1, source_target_pairs={{0,96},{32,0},{64,32},{96,64},{1,97},{33,1},{65,33},{97,65},{2,98}... | collective-permute-start | bytes 884744 | tf_op jit(solution)/shard_map/ppermute | solution.py:29
  6.2 12.6 %collective-permute-start.1 = (bf16[144,1024]{1,0:T(8,128)(2,1)S(1)}, bf16[144,1024]{1,0:T(8,128)(2,1)S(1)}, u32[]{:S(2)}, u32[]{:S(2)}) collective-permute-start(bf16[144,1024]{1,0:T(8,128)(2,1)S(1)} %get-tuple-element.63), channel_id=1, source_target_pairs={{0,64},{32,96},{64,0},{96,32},{1,65},{33,97},{65,1},{97,33},{2,66}... | collective-permute-start | bytes 884744 | tf_op jit(solution)/shard_map/ppermute | solution.py:29
  7.0 15.5 %collective-permute-start.2 = (bf16[144,1024]{1,0:T(8,128)(2,1)S(1)}, bf16[144,1024]{1,0:T(8,128)(2,1)S(1)}, u32[]{:S(2)}, u32[]{:S(2)}) collective-permute-start(bf16[144,1024]{1,0:T(8,128)(2,1)S(1)} %get-tuple-element.64), channel_id=1, source_target_pairs={{0,32},{32,64},{64,96},{96,0},{1,33},{33,65},{65,97},{97,1},{2,34}... | collective-permute-start | bytes 884744 | tf_op jit(solution)/shard_map/ppermute | solution.py:29
  25.5 40.1 %all-to-all-start = ((bf16[32,32,1024]{2,1,0:T(8,128)(2,1)}), bf16[32,32,1024]{2,1,0:T(8,128)(2,1)S(1)}, u32[]{:S(2)}, u32[]{:S(2)}) async-start(bf16[32,32,1024]{2,1,0:T(8,128)(2,1)} %bitcast.93), calls=%async_computation | async-start | bytes 4194304 | tf_op jit(solution)/shard_map/all_to_all | solution.py:460
  34.9 11.1 %collective-permute-start.5 = (bf16[128,1024]{1,0:T(8,128)(2,1)}, bf16[128,1024]{1,0:T(8,128)(2,1)}, u32[]{:S(2)}, u32[]{:S(2)}) collective-permute-start(bf16[128,1024]{1,0:T(8,128)(2,1)} %get-tuple-element.135), channel_id=1, source_target_pairs={{0,32},{32,64},{64,96},{96,0},{1,33},{33,65},{65,97},{97,1},{2,34}... | collective-permute-start | bytes 786440 | tf_op jit(solution)/shard_map/ppermute | solution.py:29
  34.9 27.1 %collective-permute-start.3 = (bf16[128,1024]{1,0:T(8,128)(2,1)}, bf16[128,1024]{1,0:T(8,128)(2,1)}, u32[]{:S(2)}, u32[]{:S(2)}) collective-permute-start(bf16[128,1024]{1,0:T(8,128)(2,1)} %get-tuple-element.137), channel_id=1, source_target_pairs={{0,96},{32,0},{64,32},{96,64},{1,97},{33,1},{65,33},{97,65},{2,98}... | collective-permute-start | bytes 786440 | tf_op jit(solution)/shard_map/ppermute | solution.py:29
  40.8 21.2 %collective-permute-start.4 = (bf16[128,1024]{1,0:T(8,128)(2,1)}, bf16[128,1024]{1,0:T(8,128)(2,1)S(1)}, u32[]{:S(2)}, u32[]{:S(2)}) collective-permute-start(bf16[128,1024]{1,0:T(8,128)(2,1)} %get-tuple-element.66), channel_id=1, source_target_pairs={{0,64},{32,96},{64,0},{96,32},{1,65},{33,97},{65,1},{97,33},{2,66}... | collective-permute-start | bytes 786440 | tf_op jit(solution)/shard_map/ppermute | solution.py:29
  41.1 24.6 %copy-start.6 = (bf16[512,1024]{1,0:T(8,128)(2,1)}, bf16[512,1024]{1,0:T(8,128)(2,1)S(1)}, u32[]{:S(2)}) copy-start(bf16[512,1024]{1,0:T(8,128)(2,1)S(1)} %fusion.2.place_ref) | copy-start | bytes 3145732
  41.1 21.0 %copy-start.8 = (bf16[1024,512]{1,0:T(8,128)(2,1)S(1)}, bf16[1024,512]{1,0:T(8,128)(2,1)}, u32[]{:S(2)}) copy-start(bf16[1024,512]{1,0:T(8,128)(2,1)} %copy-done.7) | copy-start | bytes 3145732
  42.5 29.9 %collective-permute-start.14 = (bf16[256,1024]{1,0:T(8,128)(2,1)}, bf16[256,1024]{1,0:T(8,128)(2,1)}, u32[]{:S(2)}, u32[]{:S(2)}) collective-permute-start(bf16[256,1024]{1,0:T(8,128)(2,1)} %get-tuple-element.71), channel_id=1, source_target_pairs={{0,64},{32,96},{64,0},{96,32},{1,65},{33,97},{65,1},{97,33},{2,66}... | collective-permute-start | bytes 1572872 | tf_op jit(solution)/shard_map/ppermute | solution.py:29
  46.0 27.3 %collective-permute-start.13 = (bf16[256,1024]{1,0:T(8,128)(2,1)}, bf16[256,1024]{1,0:T(8,128)(2,1)}, u32[]{:S(2)}, u32[]{:S(2)}) collective-permute-start(bf16[256,1024]{1,0:T(8,128)(2,1)} %get-tuple-element.70), channel_id=1, source_target_pairs={{0,96},{32,0},{64,32},{96,64},{1,97},{33,1},{65,33},{97,65},{2,98}... | collective-permute-start | bytes 1572872 | tf_op jit(solution)/shard_map/ppermute | solution.py:29
  46.0 27.3 %collective-permute-start.15 = (bf16[256,1024]{1,0:T(8,128)(2,1)}, bf16[256,1024]{1,0:T(8,128)(2,1)}, u32[]{:S(2)}, u32[]{:S(2)}) collective-permute-start(bf16[256,1024]{1,0:T(8,128)(2,1)} %get-tuple-element.72), channel_id=1, source_target_pairs={{0,32},{32,64},{64,96},{96,0},{1,33},{33,65},{65,97},{97,1},{2,34}... | collective-permute-start | bytes 1572872 | tf_op jit(solution)/shard_map/ppermute | solution.py:29
  68.6 26.9 %collective-permute-start.7 = (bf16[512,1024]{1,0:T(8,128)(2,1)}, bf16[512,1024]{1,0:T(8,128)(2,1)}, u32[]{:S(2)}, u32[]{:S(2)}) collective-permute-start(bf16[512,1024]{1,0:T(8,128)(2,1)} %shard_map.129.refs_0_), channel_id=1, source_target_pairs={{0,32},{32,64},{64,96},{96,0},{1,33},{33,65},{65,97},{97,1},{2,34}... | collective-permute-start | bytes 3145736 | tf_op jit(solution)/shard_map/ppermute | solution.py:29
  68.6 28.0 %collective-permute-start.6 = (bf16[512,1024]{1,0:T(8,128)(2,1)}, bf16[512,1024]{1,0:T(8,128)(2,1)}, u32[]{:S(2)}, u32[]{:S(2)}) collective-permute-start(bf16[512,1024]{1,0:T(8,128)(2,1)} %shard_map.129.refs_0_), channel_id=1, source_target_pairs={{0,96},{32,0},{64,32},{96,64},{1,97},{33,1},{65,33},{97,65},{2,98}... | collective-permute-start | bytes 3145736 | tf_op jit(solution)/shard_map/ppermute | solution.py:29
  73.3 45.4 %all-to-all-start.1 = ((bf16[32,32,1024]{2,1,0:T(8,128)(2,1)}), bf16[32,32,1024]{2,1,0:T(8,128)(2,1)}, u32[]{:S(2)}, u32[]{:S(2)}) async-start(bf16[32,32,1024]{2,1,0:T(8,128)(2,1)} %bitcast.97), calls=%async_computation.1 | async-start | bytes 4194304 | tf_op jit(solution)/shard_map/all_to_all | solution.py:460
  96.6 14.0 %collective-permute-start.8 = (bf16[256,1024]{1,0:T(8,128)(2,1)S(1)}, bf16[256,1024]{1,0:T(8,128)(2,1)S(1)}, u32[]{:S(2)}, u32[]{:S(2)}) collective-permute-start(bf16[256,1024]{1,0:T(8,128)(2,1)S(1)} %slice.141), channel_id=1, source_target_pairs={{0,32},{32,64},{64,96},{96,0},{1,33},{33,65},{65,97},{97,1},{2,34}... | collective-permute-start | bytes 1572872 | tf_op jit(solution)/shard_map/ppermute | solution.py:29
  97.8 13.2 %collective-permute-start.9 = (bf16[256,1024]{1,0:T(8,128)(2,1)S(1)}, bf16[256,1024]{1,0:T(8,128)(2,1)S(1)}, u32[]{:S(2)}, u32[]{:S(2)}) collective-permute-start(bf16[256,1024]{1,0:T(8,128)(2,1)S(1)} %slice.142), channel_id=1, source_target_pairs={{0,96},{32,0},{64,32},{96,64},{1,97},{33,1},{65,33},{97,65},{2,98}... | collective-permute-start | bytes 1572872 | tf_op jit(solution)/shard_map/ppermute | solution.py:29
  113.2 26.0 %copy-start.21 = (bf16[512,256]{1,0:T(8,128)(2,1)}, bf16[512,256]{1,0:T(8,128)(2,1)S(1)}, u32[]{:S(2)}) copy-start(bf16[512,256]{1,0:T(8,128)(2,1)S(1)} %get-tuple-element.95.refs_0_.refs_4_) | copy-start | bytes 786436
  113.2 13.1 %collective-permute-start.12 = (bf16[512,256]{1,0:T(8,128)(2,1)S(1)}, bf16[512,256]{1,0:T(8,128)(2,1)S(1)}, u32[]{:S(2)}, u32[]{:S(2)}) collective-permute-start(bf16[512,256]{1,0:T(8,128)(2,1)S(1)} %get-tuple-element.95.refs_0_.refs_4_), channel_id=1, source_target_pairs={{0,32},{32,64},{64,96},{96,0},{1,33},{33,65},{65,97},{97,1},{2,34}... | collective-permute-start | bytes 786440 | tf_op jit(solution)/shard_map/ppermute | solution.py:29
  114.4 17.3 %copy-start.11 = (f32[512,1]{1,0:T(8,128)}, f32[512,1]{1,0:T(8,128)S(1)}, u32[]{:S(2)}) copy-start(f32[512,1]{1,0:T(8,128)S(1)} %copy.30.refs_8_.refs_7_) | copy-start | bytes 6148
  114.4 17.0 %collective-permute-start.11 = (bf16[512,256]{1,0:T(8,128)(2,1)S(1)}, bf16[512,256]{1,0:T(8,128)(2,1)S(1)}, u32[]{:S(2)}, u32[]{:S(2)}) collective-permute-start(bf16[512,256]{1,0:T(8,128)(2,1)S(1)} %get-tuple-element.95.refs_0_.refs_4_), channel_id=1, source_target_pairs={{0,64},{32,96},{64,0},{96,32},{1,65},{33,97},{65,1},{97,33},{2,66}... | collective-permute-start | bytes 786440 | tf_op jit(solution)/shard_map/ppermute | solution.py:29
  118.7 13.0 %collective-permute-start.10 = (bf16[512,256]{1,0:T(8,128)(2,1)S(1)}, bf16[512,256]{1,0:T(8,128)(2,1)S(1)}, u32[]{:S(2)}, u32[]{:S(2)}) collective-permute-start(bf16[512,256]{1,0:T(8,128)(2,1)S(1)} %get-tuple-element.95.refs_0_.refs_4_), channel_id=1, source_target_pairs={{0,96},{32,0},{64,32},{96,64},{1,97},{33,1},{65,33},{97,65},{2,98}... | collective-permute-start | bytes 786440 | tf_op jit(solution)/shard_map/ppermute | solution.py:29
  118.7 13.0 %copy-start.9 = (bf16[1024,512]{1,0:T(8,128)(2,1)S(1)}, bf16[1024,512]{1,0:T(8,128)(2,1)}, u32[]{:S(2)}) copy-start(bf16[1024,512]{1,0:T(8,128)(2,1)} %fusion.3.refs_9_.place_ref) | copy-start | bytes 3145732
  118.7 13.0 %copy-start.20 = (bf16[256,1024]{1,0:T(8,128)(2,1)S(1)}, bf16[256,1024]{1,0:T(8,128)(2,1)}, u32[]{:S(2)}) copy-start(bf16[256,1024]{1,0:T(8,128)(2,1)} %get-tuple-element.69.refs_0_.refs_4_) | copy-start | bytes 1572868
  124.2 14.7 %collective-permute-start.18 = (bf16[512,256]{1,0:T(8,128)(2,1)S(1)}, bf16[512,256]{1,0:T(8,128)(2,1)S(1)}, u32[]{:S(2)}, u32[]{:S(2)}) collective-permute-start(bf16[512,256]{1,0:T(8,128)(2,1)S(1)} %get-tuple-element.75), channel_id=1, source_target_pairs={{0,32},{32,64},{64,96},{96,0},{1,33},{33,65},{65,97},{97,1},{2,34}... | collective-permute-start | bytes 786440 | tf_op jit(solution)/shard_map/ppermute | solution.py:29
  126.2 13.0 %collective-permute-start.17 = (bf16[512,256]{1,0:T(8,128)(2,1)S(1)}, bf16[512,256]{1,0:T(8,128)(2,1)S(1)}, u32[]{:S(2)}, u32[]{:S(2)}) collective-permute-start(bf16[512,256]{1,0:T(8,128)(2,1)S(1)} %get-tuple-element.76), channel_id=1, source_target_pairs={{0,64},{32,96},{64,0},{96,32},{1,65},{33,97},{65,1},{97,33},{2,66}... | collective-permute-start | bytes 786440 | tf_op jit(solution)/shard_map/ppermute | solution.py:29
  126.3 12.5 %copy-start.24 = (bf16[512,256]{1,0:T(8,128)(2,1)}, bf16[512,256]{1,0:T(8,128)(2,1)S(1)}, u32[]{:S(2)}) copy-start(bf16[512,256]{1,0:T(8,128)(2,1)S(1)} %collective-permute-done.12.refs_3_) | copy-start | bytes 786436
  126.3 12.6 %collective-permute-start.16 = (bf16[512,256]{1,0:T(8,128)(2,1)S(1)}, bf16[512,256]{1,0:T(8,128)(2,1)S(1)}, u32[]{:S(2)}, u32[]{:S(2)}) collective-permute-start(bf16[512,256]{1,0:T(8,128)(2,1)S(1)} %get-tuple-element.77), channel_id=1, source_target_pairs={{0,96},{32,0},{64,32},{96,64},{1,97},{33,1},{65,33},{97,65},{2,98}... | collective-permute-start | bytes 786440 | tf_op jit(solution)/shard_map/ppermute | solution.py:29
  145.6 24.9 %collective-permute-start.19 = (bf16[512,1024]{1,0:T(8,128)(2,1)}, bf16[512,1024]{1,0:T(8,128)(2,1)}, u32[]{:S(2)}, u32[]{:S(2)}) collective-permute-start(bf16[512,1024]{1,0:T(8,128)(2,1)} %get-tuple-element.86), channel_id=1, source_target_pairs={{0,32},{32,64},{64,96},{96,0},{1,33},{33,65},{65,97},{97,1},{2,34}... | collective-permute-start | bytes 3145736 | tf_op jit(solution)/shard_map/ppermute | solution.py:29
  147.4 25.7 %collective-permute-start.20 = (bf16[512,1024]{1,0:T(8,128)(2,1)}, bf16[512,1024]{1,0:T(8,128)(2,1)}, u32[]{:S(2)}, u32[]{:S(2)}) collective-permute-start(bf16[512,1024]{1,0:T(8,128)(2,1)} %get-tuple-element.87), channel_id=1, source_target_pairs={{0,96},{32,0},{64,32},{96,64},{1,97},{33,1},{65,33},{97,65},{2,98}... | collective-permute-start | bytes 3145736 | tf_op jit(solution)/shard_map/ppermute | solution.py:29
  149.6 45.8 %all-to-all-start.2 = ((bf16[32,32,1024]{2,1,0:T(8,128)(2,1)}), bf16[32,32,1024]{2,1,0:T(8,128)(2,1)}, u32[]{:S(2)}, u32[]{:S(2)}) async-start(bf16[32,32,1024]{2,1,0:T(8,128)(2,1)} %bitcast.96), calls=%async_computation.2 | async-start | bytes 4194304 | tf_op jit(solution)/shard_map/all_to_all | solution.py:460
  161.4 16.6 %copy-start.34 = (f32[512,1]{1,0:T(8,128)S(1)}, f32[512,1]{1,0:T(8,128)}, u32[]{:S(2)}) copy-start(f32[512,1]{1,0:T(8,128)} %get-tuple-element.94) | copy-start | bytes 6148
  161.4 16.7 %copy-start.22 = (bf16[512,256]{1,0:T(8,128)(2,1)S(1)}, bf16[512,256]{1,0:T(8,128)(2,1)}, u32[]{:S(2)}) copy-start(bf16[512,256]{1,0:T(8,128)(2,1)} %copy-done.21) | copy-start | bytes 786436
  161.4 16.7 %copy-start.25 = (bf16[512,256]{1,0:T(8,128)(2,1)S(1)}, bf16[512,256]{1,0:T(8,128)(2,1)}, u32[]{:S(2)}) copy-start(bf16[512,256]{1,0:T(8,128)(2,1)} %copy-done.24) | copy-start | bytes 786436
  161.4 16.7 %copy-start.27 = (bf16[512,256]{1,0:T(8,128)(2,1)S(1)}, bf16[512,256]{1,0:T(8,128)(2,1)}, u32[]{:S(2)}) copy-start(bf16[512,256]{1,0:T(8,128)(2,1)} %copy-done.26) | copy-start | bytes 786436
  161.4 16.7 %copy-start.29 = (bf16[512,256]{1,0:T(8,128)(2,1)S(1)}, bf16[512,256]{1,0:T(8,128)(2,1)}, u32[]{:S(2)}) copy-start(bf16[512,256]{1,0:T(8,128)(2,1)} %copy-done.28) | copy-start | bytes 786436
  172.7 14.4 %collective-permute-start.24 = (bf16[256,1024]{1,0:T(8,128)(2,1)}, bf16[256,1024]{1,0:T(8,128)(2,1)S(1)}, u32[]{:S(2)}, u32[]{:S(2)}) collective-permute-start(bf16[256,1024]{1,0:T(8,128)(2,1)} %add_convert_fusion.1), channel_id=1, source_target_pairs={{0,32},{32,64},{64,96},{96,0},{1,33},{33,65},{65,97},{97,1},{2,34}... | collective-permute-start | bytes 1572872 | tf_op jit(solution)/shard_map/ppermute | solution.py:29
  175.1 15.4 %collective-permute-start.25 = (bf16[256,1024]{1,0:T(8,128)(2,1)}, bf16[256,1024]{1,0:T(8,128)(2,1)}, u32[]{:S(2)}, u32[]{:S(2)}) collective-permute-start(bf16[256,1024]{1,0:T(8,128)(2,1)} %add_convert_fusion), channel_id=1, source_target_pairs={{0,96},{32,0},{64,32},{96,64},{1,97},{33,1},{65,33},{97,65},{2,98}... | collective-permute-start | bytes 1572872 | tf_op jit(solution)/shard_map/ppermute | solution.py:29
  182.0 29.2 %collective-permute-start.28 = (bf16[256,1024]{1,0:T(8,128)(2,1)}, bf16[256,1024]{1,0:T(8,128)(2,1)S(1)}, u32[]{:S(2)}, u32[]{:S(2)}) collective-permute-start(bf16[256,1024]{1,0:T(8,128)(2,1)} %get-tuple-element.118), channel_id=1, source_target_pairs={{0,32},{32,64},{64,96},{96,0},{1,33},{33,65},{65,97},{97,1},{2,34}... | collective-permute-start | bytes 1572872 | tf_op jit(solution)/shard_map/ppermute | solution.py:29
  182.0 30.5 %collective-permute-start.26 = (bf16[256,1024]{1,0:T(8,128)(2,1)}, bf16[256,1024]{1,0:T(8,128)(2,1)S(1)}, u32[]{:S(2)}, u32[]{:S(2)}) collective-permute-start(bf16[256,1024]{1,0:T(8,128)(2,1)} %get-tuple-element.120), channel_id=1, source_target_pairs={{0,96},{32,0},{64,32},{96,64},{1,97},{33,1},{65,33},{97,65},{2,98}... | collective-permute-start | bytes 1572872 | tf_op jit(solution)/shard_map/ppermute | solution.py:29
  195.4 37.8 %all-to-all-start.3 = ((bf16[32,32,1024]{2,1,0:T(8,128)(2,1)}), bf16[32,32,1024]{2,1,0:T(8,128)(2,1)}, u32[]{:S(2)}, u32[]{:S(2)}) async-start(bf16[32,32,1024]{2,1,0:T(8,128)(2,1)} %bitcast.94), calls=%async_computation.3 | async-start | bytes 4194304 | tf_op jit(solution)/shard_map/all_to_all | solution.py:460
  202.6 16.9 %collective-permute-start.27 = (bf16[256,1024]{1,0:T(8,128)(2,1)S(1)}, bf16[256,1024]{1,0:T(8,128)(2,1)S(1)}, u32[]{:S(2)}, u32[]{:S(2)}) collective-permute-start(bf16[256,1024]{1,0:T(8,128)(2,1)S(1)} %copy-done.33), channel_id=1, source_target_pairs={{0,64},{32,96},{64,0},{96,32},{1,65},{33,97},{65,1},{97,33},{2,66}... | collective-permute-start | bytes 1572872 | tf_op jit(solution)/shard_map/ppermute | solution.py:29
  207.9 17.4 %collective-permute-start.23 = (bf16[144,1024]{1,0:T(8,128)(2,1)S(1)}, bf16[144,1024]{1,0:T(8,128)(2,1)S(1)}, u32[]{:S(2)}, u32[]{:S(2)}) collective-permute-start(bf16[144,1024]{1,0:T(8,128)(2,1)S(1)} %get-tuple-element.146), channel_id=1, source_target_pairs={{0,32},{32,64},{64,96},{96,0},{1,33},{33,65},{65,97},{97,1},{2,34}... | collective-permute-start | bytes 884744 | tf_op jit(solution)/shard_map/ppermute | solution.py:29
  210.3 15.6 %collective-permute-start.21 = (bf16[144,1024]{1,0:T(8,128)(2,1)S(1)}, bf16[144,1024]{1,0:T(8,128)(2,1)S(1)}, u32[]{:S(2)}, u32[]{:S(2)}) collective-permute-start(bf16[144,1024]{1,0:T(8,128)(2,1)S(1)} %get-tuple-element.147), channel_id=1, source_target_pairs={{0,96},{32,0},{64,32},{96,64},{1,97},{33,1},{65,33},{97,65},{2,98}... | collective-permute-start | bytes 884744 | tf_op jit(solution)/shard_map/ppermute | solution.py:29
  211.2 19.7 %collective-permute-start.22 = (bf16[144,1024]{1,0:T(8,128)(2,1)S(1)}, bf16[144,1024]{1,0:T(8,128)(2,1)S(1)}, u32[]{:S(2)}, u32[]{:S(2)}) collective-permute-start(bf16[144,1024]{1,0:T(8,128)(2,1)S(1)} %get-tuple-element.148), channel_id=1, source_target_pairs={{0,64},{32,96},{64,0},{96,32},{1,65},{33,97},{65,1},{97,33},{2,66}... | collective-permute-start | bytes 884744 | tf_op jit(solution)/shard_map/ppermute | solution.py:29
  236.1 9.7 %collective-permute-start.31 = (bf16[128,1024]{1,0:T(8,128)(2,1)S(1)}, bf16[128,1024]{1,0:T(8,128)(2,1)S(1)}, u32[]{:S(2)}, u32[]{:S(2)}) collective-permute-start(bf16[128,1024]{1,0:T(8,128)(2,1)S(1)} %get-tuple-element.126), channel_id=1, source_target_pairs={{0,32},{32,64},{64,96},{96,0},{1,33},{33,65},{65,97},{97,1},{2,34}... | collective-permute-start | bytes 786440 | tf_op jit(solution)/shard_map/ppermute | solution.py:29
  237.0 15.0 %collective-permute-start.30 = (bf16[128,1024]{1,0:T(8,128)(2,1)S(1)}, bf16[128,1024]{1,0:T(8,128)(2,1)S(1)}, u32[]{:S(2)}, u32[]{:S(2)}) collective-permute-start(bf16[128,1024]{1,0:T(8,128)(2,1)S(1)} %get-tuple-element.127), channel_id=1, source_target_pairs={{0,64},{32,96},{64,0},{96,32},{1,65},{33,97},{65,1},{97,33},{2,66}... | collective-permute-start | bytes 786440 | tf_op jit(solution)/shard_map/ppermute | solution.py:29
  240.9 11.2 %collective-permute-start.29 = (bf16[128,1024]{1,0:T(8,128)(2,1)S(1)}, bf16[128,1024]{1,0:T(8,128)(2,1)S(1)}, u32[]{:S(2)}, u32[]{:S(2)}) collective-permute-start(bf16[128,1024]{1,0:T(8,128)(2,1)S(1)} %get-tuple-element.128), channel_id=1, source_target_pairs={{0,96},{32,0},{64,32},{96,64},{1,97},{33,1},{65,33},{97,65},{2,98}... | collective-permute-start | bytes 786440 | tf_op jit(solution)/shard_map/ppermute | solution.py:29
  (24 other events, 135.1 us)
